TPU v7x, 128 devices: a whole 4x4x4 slice. The times are simulated.
128 devices in a mesh: row: 16 (over x, z_hi, core), rep: 8 (over z_lo, y).
Axes of the slice: x: 4, y: 4, z: 4 (z_hi: 2, z_lo: 2; z = z_hi * 2 + z_lo), core: 2. Of those that a mesh axis runs over, the one named last changes fastest.
Arguments:
- features: bfloat16 [32768, 256], P('row'), may hold values from -6 to 6
- weight: bfloat16 [256, 256], replicated, may hold values from -0.375 to 0.375
- tile_values: bfloat16 [16, 8, 2, 192, 128, 128], P('row', 'rep'), may hold values from -0.0546875 to 0.0546875
- tile_rows: int32 [16, 8, 2, 192], P('row', 'rep'), may hold values from 0 to 15, as said below
- tile_cols: int32 [16, 8, 2, 192], P('row', 'rep'), may hold values from 0 to 15, as said below
- tile_count: int32 [16, 8, 2], P('row', 'rep'), may hold values from 24 to 192
- train_mask: int32 [32768], P(('row', 'rep')), may hold values 0 or 1
- upstream: bfloat16 [32768, 256], P(('row', 'rep')), may hold values from -24 to 24
Outputs:
- activated: bfloat16 [32768, 256], P(('row', 'rep'))
- weight_grad: float32 [256, 256], replicated
- feature_grad: bfloat16 [32768, 256], P(('row', 'rep'))
Inputs may be any that keep to these rules, and one draw needn't show every extreme that they name: Within one list of 192 slots no pair (tile_rows, tile_cols) repeats. `tile_cols`: paired slot by slot with tile_rows.
All inputs are finite; a program needn't handle non-finite values. No bound on the sum of `train_mask` on one device may be relied on, other than what follows from the above.
Results may differ from a plain program's by a relative error of at most 0.025.
Values may be sent and summed in bfloat16 or wider, within the bound.
No kernel may reach another device: no remote copies, remote signals or barrier semaphores. Data moves between devices by JAX's collectives and lax.ppermute only.
A program may use at most 128 MiB of HBM per device.

v0:
```python
import math

import jax
import jax.numpy as jnp
from jax import lax
from jax.sharding import PartitionSpec as P

TB = 16


def passed_along(shard, axis, by):
    size = lax.axis_size(axis)
    return lax.ppermute(shard, axis, [(i, (i + by) % size) for i in range(size)])


def dense_block(tile_block, row_index, col_index, count):
    slots = tile_block.shape[0]
    edge = tile_block.shape[1]
    live = jnp.arange(slots, dtype=jnp.int32) < count
    zeroed = jnp.where(live[:, None, None], tile_block, jnp.zeros((), tile_block.dtype))
    empty = jnp.zeros((TB, TB, edge, edge), tile_block.dtype)
    return empty.at[row_index, col_index].add(zeroed)


def dense_apply(dense, source, transpose):
    edge = dense.shape[2]
    width = source.shape[1]
    pieces = source.reshape(TB, edge, width)
    if transpose:
        result = jnp.einsum("abij,aif->bjf", dense, pieces, preferred_element_type=jnp.float32)
    else:
        result = jnp.einsum("abij,bjf->aif", dense, pieces, preferred_element_type=jnp.float32)
    return result.reshape(TB * edge, width)


def per_device(
    features, weight, tile_values, tile_rows, tile_cols, tile_count, train_mask, upstream
):
    row_devices = lax.axis_size("row")
    rep_devices = lax.axis_size("rep")
    sections = row_devices // rep_devices
    replica = lax.axis_index("rep")
    tile_block = tile_values[0, 0]
    row_lists = tile_rows[0, 0]
    col_lists = tile_cols[0, 0]
    counts = tile_count[0, 0]
    block_rows = features.shape[0]
    share_rows = block_rows // rep_devices
    bit_count = (rep_devices - 1).bit_length()
    denses = [
        dense_block(
            tile_block[step_index], row_lists[step_index], col_lists[step_index], counts[step_index]
        )
        for step_index in range(sections)
    ]
    panel = features
    for bit_index in range(bit_count):
        moved = passed_along(panel, "row", (1 << bit_index) * sections)
        panel = jnp.where(replica >> bit_index & 1 == 1, moved, panel)
    partial_value = jnp.zeros((block_rows, features.shape[1]), jnp.float32)
    for step_index in range(sections):
        partial_value = partial_value + dense_apply(denses[step_index], panel, False)
        if step_index + 1 < sections:
            panel = passed_along(panel, "row", 1)
    start = replica * share_rows
    summed = lax.psum(partial_value.astype(jnp.bfloat16), "rep").astype(jnp.float32)
    share = lax.dynamic_slice_in_dim(summed, start, share_rows, 0)
    aggregate = share.astype(jnp.bfloat16)
    logits = jnp.dot(aggregate, weight, preferred_element_type=jnp.float32)
    sigmoid_part = jax.nn.sigmoid(logits)
    activated = (logits * sigmoid_part).astype(jnp.bfloat16)
    slope = sigmoid_part * (1.0 + logits * (1.0 - sigmoid_part))
    masked = (
        upstream.astype(jnp.float32) * train_mask.astype(jnp.float32)[:, None] * slope
    ).astype(jnp.bfloat16)
    local_term = jnp.dot(aggregate.T, masked, preferred_element_type=jnp.float32)
    weight_grad = lax.psum(local_term, ("row", "rep")) * (1.0 / math.sqrt(block_rows * row_devices))
    back_share = jnp.dot(masked, weight.T, preferred_element_type=jnp.float32).astype(jnp.bfloat16)
    back_block = lax.all_gather(back_share, "rep", axis=0, tiled=True)
    carried_sum = jnp.zeros((block_rows, features.shape[1]), jnp.float32)
    for step_index in range(sections):
        carried_sum = carried_sum + dense_apply(denses[step_index], back_block, True)
        carried_sum = passed_along(carried_sum.astype(jnp.bfloat16), "row", 1).astype(
            carried_sum.dtype
        )
    homeward = (replica + 1) % rep_devices
    for bit_index in range(bit_count):
        moved = passed_along(
            carried_sum.astype(jnp.bfloat16), "row", -(1 << bit_index) * sections
        ).astype(carried_sum.dtype)
        carried_sum = jnp.where(homeward >> bit_index & 1 == 1, moved, carried_sum)
    grad_total = lax.psum(carried_sum.astype(jnp.bfloat16), "rep").astype(jnp.float32)
    grad_share = lax.dynamic_slice_in_dim(grad_total, start, share_rows, 0)
    return (activated, weight_grad, grad_share.astype(jnp.bfloat16))


def solution(mesh):
    placed = (
        P("row", None),
        P(),
        P("row", "rep", None, None, None, None),
        P("row", "rep", None, None),
        P("row", "rep", None, None),
        P("row", "rep", None),
        P(("row", "rep")),
        P(("row", "rep"), None),
    )
    return jax.shard_map(
        per_device,
        mesh=mesh,
        in_specs=placed,
        out_specs=(P(("row", "rep"), None), P(), P(("row", "rep"), None)),
        check_vma=False,
    )
```

profile of v0, /device:TPU:8, one launch (start us, length us, event | category | flops | bytes accessed | tf_op | source)
XLA Modules:
  0.0 672.8 jit_solution(7163070899715114877)
XLA Ops:
  11.2 25.6 %collective-permute-done = bf16[2048,256]{1,0:T(8,128)(2,1)S(1)} collective-permute-done((bf16[2048,256]{1,0:T(8,128)(2,1)}, bf16[2048,256]{1,0:T(8,128)(2,1)S(1)}, u32[]{:S(2)}, u32[]{:S(2)}) %collective-permute-start) | collective-permute-done | bytes 1048608 | tf_op jit(solution)/shard_map/ppermute | solution.py:13
  37.0 25.5 %collective-permute-done.1 = bf16[2048,256]{1,0:T(8,128)(2,1)S(1)} collective-permute-done((bf16[2048,256]{1,0:T(8,128)(2,1)S(1)}, bf16[2048,256]{1,0:T(8,128)(2,1)S(1)}, u32[]{:S(2)}, u32[]{:S(2)}) %collective-permute-start.1) | collective-permute-done | bytes 1048608 | tf_op jit(solution)/shard_map/ppermute | solution.py:13
  64.6 23.0 %collective-permute-done.2 = bf16[2048,256]{1,0:T(8,128)(2,1)S(1)} collective-permute-done((bf16[2048,256]{1,0:T(8,128)(2,1)S(1)}, bf16[2048,256]{1,0:T(8,128)(2,1)S(1)}, u32[]{:S(2)}, u32[]{:S(2)}) %collective-permute-start.2) | collective-permute-done | bytes 1048608 | tf_op jit(solution)/shard_map/ppermute | solution.py:13
  87.9 10.4 %bitcast_select_fusion.1 = (bf16[192,128,128]{2,1,0:T(8,128)(2,1)}, bf16[192,128,128]{2,1,0:T(8,128)(2,1)}) fusion(bf16[1,1,2,192,128,128]{5,4,3,2,1,0:T(8,128)(2,1)} %param.10, pred[192]{0:T(512)(128)(4,1)S(1)} %get-tuple-element.12, pred[192]{0:T(512)(128)(4,1)S(1)} %get-tuple-element.11), kind=kLoop, calls=%fused_computation.7 | loop fusion | flops 6291456 | bytes 25166208 | tf_op jit(solution)/shard_map/jit(_where)/select_n | solution.py:20
  98.2 5.4 broadcast.78.clone
  103.6 39.9 %scatter_fusion.1 = bf16[16,16,128,128]{3,2,1,0:T(8,128)(2,1)} fusion(bf16[16,16,128,128]{3,2,1,0:T(8,128)(2,1)} %broadcast.78.clone, s32[192]{0:T(256)S(1)} %bitcast.58, bf16[192,128,128]{2,1,0:T(8,128)(2,1)} %get-tuple-element.4), kind=kCustom, calls=%fused_computation.1 | custom fusion | flops 3145728 | bytes 18875904 | tf_op jit(solution)/shard_map/scatter-add | solution.py:22
  143.5 13.7 %copy.15 = bf16[16,128,16,128]{3,2,1,0:T(8,128)(2,1)} copy(bf16[16,128,16,128]{3,1,2,0:T(8,128)(2,1)} %bitcast.55) | data formatting | bytes 16777216 | tf_op jit(solution)/shard_map/abij,bjf->aif/dot_general | solution.py:32
  157.2 5.4 broadcast.78.clone.1
  162.6 40.1 %scatter_fusion = bf16[16,16,128,128]{3,2,1,0:T(8,128)(2,1)} fusion(bf16[16,16,128,128]{3,2,1,0:T(8,128)(2,1)} %broadcast.78.clone.1, s32[192]{0:T(256)S(1)} %bitcast.57, bf16[192,128,128]{2,1,0:T(8,128)(2,1)} %get-tuple-element.3), kind=kCustom, calls=%fused_computation | custom fusion | flops 3145728 | bytes 18875904 | tf_op jit(solution)/shard_map/scatter-add | solution.py:22
  202.7 13.7 %copy.13 = bf16[16,128,16,128]{3,2,1,0:T(8,128)(2,1)} copy(bf16[16,128,16,128]{3,1,2,0:T(8,128)(2,1)} %bitcast.53) | data formatting | bytes 16777216 | tf_op jit(solution)/shard_map/abij,bjf->aif/dot_general | solution.py:32
  216.4 6.1 fusion.7
  226.3 77.7 %all-reduce.4.cloned.1.call-done = bf16[2048,256]{1,0:T(8,128)(2,1)} async-done(((bf16[2048,256]{1,0:T(8,128)(2,1)}), bf16[2048,256]{1,0:T(8,128)(2,1)}) %all-reduce.4.cloned.1.call-update) | async-done | bytes 1048592 | tf_op jit(solution)/shard_map/psum | solution.py:66
  306.7 12.4 %copy.21 = bf16[16,128,16,128]{3,1,0,2:T(8,128)(2,1)} copy(bf16[16,128,16,128]{1,3,0,2:T(8,128)(2,1)} %bitcast.54) | data formatting | bytes 16777216 | tf_op jit(solution)/shard_map/abij,aif->bjf/dot_general | solution.py:30
  319.1 25.8 %all-gather.2.cloned.1.call-done = bf16[2048,256]{1,0:T(8,128)(2,1)} async-done(((bf16[256,256]{1,0:T(8,128)(2,1)}), bf16[2048,256]{1,0:T(8,128)(2,1)}) %all-gather.2.cloned.1.call-update) | async-done | bytes 1048592 | tf_op jit(solution)/shard_map/all_gather | solution.py:79
  344.9 5.9 fusion.16
  350.9 12.5 %copy.22 = bf16[16,128,16,128]{3,1,0,2:T(8,128)(2,1)} copy(bf16[16,128,16,128]{1,3,0,2:T(8,128)(2,1)} %bitcast.56) | data formatting | bytes 16777216 | tf_op jit(solution)/shard_map/abij,aif->bjf/dot_general | solution.py:30
  363.4 5.4 collective-permute-done.4
  368.8 4.9 add_convert_fusion
  373.8 17.9 %collective-permute-done.5 = bf16[2048,256]{1,0:T(8,128)(2,1)S(1)} collective-permute-done((bf16[2048,256]{1,0:T(8,128)(2,1)S(1)}, bf16[2048,256]{1,0:T(8,128)(2,1)S(1)}, u32[]{:S(2)}, u32[]{:S(2)}) %collective-permute-start.5) | collective-permute-done | bytes 1048608 | tf_op jit(solution)/shard_map/ppermute | solution.py:13
  392.5 21.5 %collective-permute-done.6 = bf16[2048,256]{1,0:T(8,128)(2,1)S(1)} collective-permute-done((bf16[2048,256]{1,0:T(8,128)(2,1)S(1)}, bf16[2048,256]{1,0:T(8,128)(2,1)S(1)}, u32[]{:S(2)}, u32[]{:S(2)}) %collective-permute-start.6) | collective-permute-done | bytes 1048608 | tf_op jit(solution)/shard_map/ppermute | solution.py:13
  417.0 21.1 %collective-permute-done.7 = bf16[2048,256]{1,0:T(8,128)(2,1)S(1)} collective-permute-done((bf16[2048,256]{1,0:T(8,128)(2,1)}, bf16[2048,256]{1,0:T(8,128)(2,1)S(1)}, u32[]{:S(2)}, u32[]{:S(2)}) %collective-permute-start.7) | collective-permute-done | bytes 1048608 | tf_op jit(solution)/shard_map/ppermute | solution.py:13
  442.3 20.9 %collective-permute-done.8 = bf16[2048,256]{1,0:T(8,128)(2,1)} collective-permute-done((bf16[2048,256]{1,0:T(8,128)(2,1)}, bf16[2048,256]{1,0:T(8,128)(2,1)}, u32[]{:S(2)}, u32[]{:S(2)}) %collective-permute-start.8) | collective-permute-done | bytes 1048608 | tf_op jit(solution)/shard_map/ppermute | solution.py:13
  465.9 123.1 %all-reduce.6.cloned.1.call-done = f32[256,256]{1,0:T(8,128)} async-done(((f32[256,256]{1,0:T(8,128)}), f32[256,256]{1,0:T(8,128)}) %all-reduce.6.cloned.1.call-update) | async-done | bytes 262160 | tf_op jit(solution)/shard_map/psum | solution.py:77
  590.7 74.0 %all-reduce.8.cloned.1.call-done = bf16[2048,256]{1,0:T(8,128)(2,1)} async-done(((bf16[2048,256]{1,0:T(8,128)(2,1)}), bf16[2048,256]{1,0:T(8,128)(2,1)}) %all-reduce.8.cloned.1.call-update) | async-done | bytes 1048592 | tf_op jit(solution)/shard_map/psum | solution.py:92
  (50 shorter events, 27.0 us)
Async XLA Ops:
  7.2 296.8 %copy-start = (bf16[256,256]{1,0:T(8,128)(2,1)S(1)}, bf16[256,256]{1,0:T(8,128)(2,1)}, u32[]{:S(2)}) copy-start(bf16[256,256]{1,0:T(8,128)(2,1)} %param.9) | copy-start | bytes 393220
  7.2 55.5 %copy-start.4 = (s32[1,1,2]{2,1,0:T(1,128)S(1)}, s32[1,1,2]{2,1,0:T(1,128)}, u32[]{:S(2)}) copy-start(s32[1,1,2]{2,1,0:T(1,128)} %param.13) | copy-start | bytes 28
  7.2 80.6 %copy-start.3 = (s32[1,1,2,192]{3,2,1,0:T(2,128)S(1)}, s32[1,1,2,192]{3,2,1,0:T(2,128)}, u32[]{:S(2)}) copy-start(s32[1,1,2,192]{3,2,1,0:T(2,128)} %param.11) | copy-start | bytes 4612
  7.2 80.6 %copy-start.2 = (s32[1,1,2,192]{3,2,1,0:T(2,128)S(1)}, s32[1,1,2,192]{3,2,1,0:T(2,128)}, u32[]{:S(2)}) copy-start(s32[1,1,2,192]{3,2,1,0:T(2,128)} %param.12) | copy-start | bytes 4612
  7.2 296.7 %all-reduce.4.cloned.1.call-start = ((), (), s32[]{:S(2)}) async-start(), calls=%async_computation | async-start | bytes 2097152 | tf_op jit(solution)/shard_map/psum | solution.py:66
  7.3 29.5 %collective-permute-start = (bf16[2048,256]{1,0:T(8,128)(2,1)}, bf16[2048,256]{1,0:T(8,128)(2,1)S(1)}, u32[]{:S(2)}, u32[]{:S(2)}) collective-permute-start(bf16[2048,256]{1,0:T(8,128)(2,1)} %param.8), channel_id=1, source_target_pairs={{0,16},{8,24},{16,32},{24,40},{32,48},{40,56},{48,64},{56,72},{64,... | collective-permute-start | bytes 3145736 | tf_op jit(solution)/shard_map/ppermute | solution.py:13
  36.9 25.6 %collective-permute-start.1 = (bf16[2048,256]{1,0:T(8,128)(2,1)S(1)}, bf16[2048,256]{1,0:T(8,128)(2,1)S(1)}, u32[]{:S(2)}, u32[]{:S(2)}) collective-permute-start(bf16[2048,256]{1,0:T(8,128)(2,1)S(1)} %broadcast_select_fusion), channel_id=1, source_target_pairs={{0,32},{8,40},{16,48},{24,56},{32,64},{40,72},{48,80},{56,88},{64,... | collective-permute-start | bytes 3145736 | tf_op jit(solution)/shard_map/ppermute | solution.py:13
  62.6 25.0 %collective-permute-start.2 = (bf16[2048,256]{1,0:T(8,128)(2,1)S(1)}, bf16[2048,256]{1,0:T(8,128)(2,1)S(1)}, u32[]{:S(2)}, u32[]{:S(2)}) collective-permute-start(bf16[2048,256]{1,0:T(8,128)(2,1)S(1)} %broadcast_select_fusion.1), channel_id=1, source_target_pairs={{0,64},{8,72},{16,80},{24,88},{32,96},{40,104},{48,112},{56,120},{... | collective-permute-start | bytes 3145736 | tf_op jit(solution)/shard_map/ppermute | solution.py:13
  87.7 128.6 %collective-permute-start.3 = (bf16[2048,256]{1,0:T(8,128)(2,1)S(1)}, bf16[2048,256]{1,0:T(8,128)(2,1)S(1)}, u32[]{:S(2)}, u32[]{:S(2)}) collective-permute-start(bf16[2048,256]{1,0:T(8,128)(2,1)S(1)} %broadcast_select_fusion.2), channel_id=1, source_target_pairs={{0,8},{8,16},{16,24},{24,32},{32,40},{40,48},{48,56},{56,64},{64,7... | collective-permute-start | bytes 3145736 | tf_op jit(solution)/shard_map/ppermute | solution.py:13
  216.3 6.1 copy-start.1
  222.5 3.7 copy-start.5
  222.5 81.4 %copy-start.7 = (bf16[256,256]{1,0:T(8,128)(2,1)S(1)}, bf16[256,256]{1,0:T(8,128)(2,1)}, u32[]{:S(2)}) copy-start(bf16[256,256]{1,0:T(8,128)(2,1)} %param.15) | copy-start | bytes 393220
  226.2 118.7 %all-gather.2.cloned.1.call-start = ((), (), s32[]{:S(2)}) async-start(), calls=%async_computation.2 | async-start | bytes 1179648 | tf_op jit(solution)/shard_map/all_gather | solution.py:79
  306.7 282.4 %all-reduce.6.cloned.1.call-start = ((), (), s32[]{:S(2)}) async-start(), calls=%async_computation.1 | async-start | bytes 524288 | tf_op jit(solution)/shard_map/psum | solution.py:77
  350.9 17.9 %collective-permute-start.4 = (bf16[2048,256]{1,0:T(8,128)(2,1)S(1)}, bf16[2048,256]{1,0:T(8,128)(2,1)S(1)}, u32[]{:S(2)}, u32[]{:S(2)}) collective-permute-start(bf16[2048,256]{1,0:T(8,128)(2,1)S(1)} %fusion.16), channel_id=1, source_target_pairs={{0,8},{8,16},{16,24},{24,32},{32,40},{40,48},{48,56},{56,64},{64,7... | collective-permute-start | bytes 3145736 | tf_op jit(solution)/shard_map/ppermute | solution.py:13
  350.9 17.8 %copy-start.6 = (bf16[2048,256]{1,0:T(8,128)(2,1)S(1)}, bf16[2048,256]{1,0:T(8,128)(2,1)}, u32[]{:S(2)}) copy-start(bf16[2048,256]{1,0:T(8,128)(2,1)} %all-gather.2.cloned.1.call-done) | copy-start | bytes 3145732
  373.7 18.0 %collective-permute-start.5 = (bf16[2048,256]{1,0:T(8,128)(2,1)S(1)}, bf16[2048,256]{1,0:T(8,128)(2,1)S(1)}, u32[]{:S(2)}, u32[]{:S(2)}) collective-permute-start(bf16[2048,256]{1,0:T(8,128)(2,1)S(1)} %add_convert_fusion), channel_id=1, source_target_pairs={{0,8},{8,16},{16,24},{24,32},{32,40},{40,48},{48,56},{56,64},{64,7... | collective-permute-start | bytes 3145736 | tf_op jit(solution)/shard_map/ppermute | solution.py:13
  391.7 22.4 %collective-permute-start.6 = (bf16[2048,256]{1,0:T(8,128)(2,1)S(1)}, bf16[2048,256]{1,0:T(8,128)(2,1)S(1)}, u32[]{:S(2)}, u32[]{:S(2)}) collective-permute-start(bf16[2048,256]{1,0:T(8,128)(2,1)S(1)} %collective-permute-done.5), channel_id=1, source_target_pairs={{0,112},{8,120},{16,0},{24,8},{32,16},{40,24},{48,32},{56,40},{64,... | collective-permute-start | bytes 3145736 | tf_op jit(solution)/shard_map/ppermute | solution.py:13
  415.3 22.8 %collective-permute-start.7 = (bf16[2048,256]{1,0:T(8,128)(2,1)}, bf16[2048,256]{1,0:T(8,128)(2,1)S(1)}, u32[]{:S(2)}, u32[]{:S(2)}) collective-permute-start(bf16[2048,256]{1,0:T(8,128)(2,1)} %fusion.17), channel_id=1, source_target_pairs={{0,96},{8,104},{16,112},{24,120},{32,0},{40,8},{48,16},{56,24},{64... | collective-permute-start | bytes 3145736 | tf_op jit(solution)/shard_map/ppermute | solution.py:13
  439.5 23.7 %collective-permute-start.8 = (bf16[2048,256]{1,0:T(8,128)(2,1)}, bf16[2048,256]{1,0:T(8,128)(2,1)}, u32[]{:S(2)}, u32[]{:S(2)}) collective-permute-start(bf16[2048,256]{1,0:T(8,128)(2,1)} %fusion.18), channel_id=1, source_target_pairs={{0,64},{8,72},{16,80},{24,88},{32,96},{40,104},{48,112},{56,120},{... | collective-permute-start | bytes 3145736 | tf_op jit(solution)/shard_map/ppermute | solution.py:13
  442.2 222.5 %all-reduce.8.cloned.1.call-start = ((), (), s32[]{:S(2)}) async-start(), calls=%async_computation.3 | async-start | bytes 2097152 | tf_op jit(solution)/shard_map/psum | solution.py:92
Sparse Core Ops, SparseCore 0:
  226.3 77.5 all-reduce.3
  306.8 38.0 all-gather.1
  442.3 146.6 all-reduce.5
  591.4 73.2 all-reduce.7
where the time goes:
time: 676 us; the launch traced here: 673 us
  waiting for transfers between devices  462 us (68%)
  other arithmetic  101 us (15%)
  local copies, waits for them, and re-layouts  63.5 us (9%)
  matrix products  25.1 us (4%)
  between operations  14 us (2%)
  starting transfers between devices  7.95 us (1%)
    ppermute x9, waiting for transfers between devices, passed_along(): lax.ppermute(shard, axis, [(i, (i + by) % size) for i in range(size)])  161 us
    psum x1, waiting for transfers between devices, per_device(): lax.psum(local_term, ('row', 'rep'))  123 us
    scatter-add x2, other arithmetic, dense_block(): return empty.at[row_index, col_index].add(zeroed)  80 us
    psum x1, waiting for transfers between devices, per_device(): lax.psum(partial_value.astype(jnp.bfloat16), 'rep').astype(jnp.float32)  77.7 us
    psum x1, waiting for transfers between devices, per_device(): lax.psum(carried_sum.astype(jnp.bfloat16), 'rep').astype(jnp.float32)  74 us
    dot_general x2, local copies, waits for them, and re-layouts, dense_apply(): jnp.einsum('abij,bjf->aif', dense, pieces, preferred_element_type=jnp.flo...  27.4 us
    all_gather x1, waiting for transfers between devices, per_device(): back_block = lax.all_gather(back_share, 'rep', axis=0, tiled=True)  25.8 us
    dot_general x2, local copies, waits for them, and re-layouts, dense_apply(): jnp.einsum('abij,aif->bjf', dense, pieces, preferred_element_type=jnp.flo...  24.8 us
  transfers between devices with their start and end apart: 13, of which 12 were waited for; matrix products, arithmetic and copies ran while one was open for 24% of the time, Pallas kernels for 0%

commit v1 on v0

v1 whole, which is shorter than its diff:
```python
import functools
import math

import jax
import jax.numpy as jnp
from jax import lax
from jax.experimental import pallas as pl
from jax.experimental.pallas import tpu as pltpu
from jax.sharding import PartitionSpec as P

TB = 16
TILE = 128
CHUNK = 48
VMEM = pl.BlockSpec(memory_space=pltpu.VMEM)
SMEM = pl.BlockSpec(memory_space=pltpu.SMEM)
NT = (((1,), (1,)), ((), ()))
TN = (((0,), (0,)), ((), ()))


def params(mib, **more):
    return pltpu.CompilerParams(vmem_limit_bytes=mib << 20, **more)


def in_vmem(array):
    return pltpu.with_memory_space_constraint(array, pltpu.VMEM)


def build_kernel(rows, cols, count, tiles, panels):
    part, chunk = pl.program_id(0), pl.program_id(1)

    @pl.when(chunk == 0)
    def _():
        def clear(b, carry):
            panels[part, b] = jnp.zeros(panels.shape[2:], panels.dtype)
            return carry

        lax.fori_loop(0, TB, clear, 0)

    def place(t, carry):
        slot = chunk * CHUNK + t
        row = pl.multiple_of(rows[part, slot] * TILE, TILE)
        panels[part, cols[part, slot], pl.ds(row, TILE), :] = tiles[0, t]
        return carry

    lax.fori_loop(0, jnp.clip(count[part] - chunk * CHUNK, 0, CHUNK), place, 0)


def build(tile_values, tile_rows, tile_cols, tile_count):
    sections, slots = tile_rows.shape

    def block(part, chunk, rows, cols, count):
        last = lax.div(count[part] - 1, CHUNK)
        return part, jnp.minimum(chunk, last), 0, 0

    return pl.pallas_call(
        build_kernel,
        grid_spec=pltpu.PrefetchScalarGridSpec(
            num_scalar_prefetch=3,
            grid=(sections, slots // CHUNK),
            in_specs=[pl.BlockSpec((1, CHUNK, TILE, TILE), block)],
            out_specs=VMEM,
        ),
        out_shape=pltpu.VMEM((sections, TB, TB * TILE, TILE), jnp.bfloat16),
        compiler_params=params(12),
        cost_estimate=pl.CostEstimate(flops=0, bytes_accessed=30 << 20, transcendentals=0),
        name="build",
    )(tile_rows, tile_cols, tile_count, tile_values)


def wide(panels, part, rows):
    return jnp.concatenate([panels[part, b, rows, :] for b in range(TB)], axis=1)


def forward_kernel(share, mine, panels, first, second, *outs):
    for d, out in enumerate(outs):
        q = lax.rem(mine[0] + d, len(outs))
        rows = pl.ds(pl.multiple_of(q * share, share), share)
        total = jnp.dot(wide(panels, 0, rows), first[...], preferred_element_type=jnp.float32)
        total += jnp.dot(wide(panels, 1, rows), second[...], preferred_element_type=jnp.float32)
        out[...] = total.astype(out.dtype)


def forward(mine, panels, first, second, shares):
    rows, width = first.shape
    share = rows // shares
    return pl.pallas_call(
        functools.partial(forward_kernel, share),
        in_specs=[SMEM, VMEM, VMEM, VMEM],
        out_specs=[VMEM] * shares,
        out_shape=[jax.ShapeDtypeStruct((share, width), jnp.bfloat16)] * shares,
        compiler_params=params(20),
        cost_estimate=pl.CostEstimate(flops=4 * rows * rows * width, bytes_accessed=4 << 20, transcendentals=0),
        name="forward",
    )(mine, in_vmem(panels), first, second)


def middle_kernel(shares, mine, *refs):
    parts = refs[:shares]
    weight, cotangent, activated, back, term = refs[shares : shares + 5]
    sends = refs[shares + 5 :]
    total = parts[0][...].astype(jnp.float32)
    for part in parts[1:]:
        total += part[...].astype(jnp.float32)
    aggregate = total.astype(jnp.bfloat16)
    logits = jnp.dot(aggregate, weight[...], preferred_element_type=jnp.float32)
    sigmoid_part = jax.nn.sigmoid(logits)
    activated[...] = (logits * sigmoid_part).astype(jnp.bfloat16)
    slope = sigmoid_part * (1.0 + logits * (1.0 - sigmoid_part))
    masked = (cotangent[...] * slope).astype(jnp.bfloat16)
    term[...] = lax.dot_general(aggregate, masked, TN, preferred_element_type=jnp.float32)
    turned = lax.dot_general(weight[...], masked, NT, preferred_element_type=jnp.float32)
    turned = turned.astype(jnp.bfloat16)
    back[...] = turned
    width = weight.shape[0]
    some = width // shares
    for d, send in enumerate(sends, 1):
        q = lax.rem(mine[0] + d, shares)
        send[:width, :] = turned
        send[width:, :] = term[pl.ds(pl.multiple_of(q * some, some), some), :].astype(jnp.bfloat16)


def middle(mine, parts, weight, cotangent):
    shares = len(parts)
    share, width = cotangent.shape
    bf16, f32 = jnp.bfloat16, jnp.float32
    result = pl.pallas_call(
        functools.partial(middle_kernel, shares),
        in_specs=[SMEM] + [VMEM] * (shares + 2),
        out_specs=[VMEM] * (shares + 2),
        out_shape=[
            jax.ShapeDtypeStruct((share, width), bf16),
            jax.ShapeDtypeStruct((width, share), bf16),
            jax.ShapeDtypeStruct((width, width), f32),
        ]
        + [jax.ShapeDtypeStruct((width + width // shares, share), bf16)] * (shares - 1),
        compiler_params=params(12),
        name="middle",
    )(mine, *parts, weight, cotangent)
    return result[0], result[1], result[2], result[3:]


def backward_kernel(part, share, rotate, mine, panels, *refs):
    backs, out = refs[:-1], refs[-1]
    shares = len(backs)
    width = backs[0].shape[1]
    for d in range(out.shape[0]):
        q = lax.rem(mine[0] + d, shares) if rotate else d
        total = None
        for e, back in enumerate(backs):
            p = lax.rem(mine[0] + shares - e, shares)
            rows = pl.ds(pl.multiple_of(p * share, share), share)
            block = jnp.concatenate([panels[part, 2 * q + h, rows, :] for h in range(2)], axis=1)
            product = jnp.dot(back[:width, :], block, preferred_element_type=jnp.float32)
            total = product if total is None else total + product
        out[d] = total.astype(out.dtype)


def backward(part, rotate, mine, panels, backs, dtype):
    shares = len(backs)
    width = share = backs[0].shape[1]
    return pl.pallas_call(
        functools.partial(backward_kernel, part, share, rotate),
        in_specs=[SMEM] + [VMEM] * (shares + 1),
        out_specs=VMEM,
        out_shape=jax.ShapeDtypeStruct((shares, width, share), dtype),
        compiler_params=params(12),
        cost_estimate=pl.CostEstimate(flops=2 * (shares * share) ** 2 * width, bytes_accessed=3 << 20, transcendentals=0),
        name="backward",
    )(mine, in_vmem(panels), *backs)


def merge_kernel(mine, own, other, *outs):
    for d, out in enumerate(outs):
        q = lax.rem(mine[0] + d, len(outs))
        out[...] = (own[d] + other[q].astype(jnp.float32)).astype(out.dtype)


def merge(mine, own, other):
    shares, width, share = own.shape
    return pl.pallas_call(
        merge_kernel,
        in_specs=[SMEM, VMEM, VMEM],
        out_specs=[VMEM] * shares,
        out_shape=[jax.ShapeDtypeStruct((width, share), jnp.bfloat16)] * shares,
        compiler_params=params(12),
        name="merge",
    )(mine, own, other)


def finish_kernel(*refs):
    total = refs[0][...].astype(jnp.float32)
    for part in refs[1:-1]:
        total += part[...].astype(jnp.float32)
    refs[-1][...] = total.T.astype(jnp.bfloat16)


def finish(parts):
    width, share = parts[0].shape
    return pl.pallas_call(
        finish_kernel,
        in_specs=[VMEM] * len(parts),
        out_specs=VMEM,
        out_shape=jax.ShapeDtypeStruct((share, width), jnp.bfloat16),
        compiler_params=params(12),
        name="finish",
    )(*parts)


def pairs(row_devices, rep_devices, target):
    found = []
    for i in range(row_devices):
        for r in range(rep_devices):
            j, q = target(i, r)
            found.append((i * rep_devices + r, (j % row_devices) * rep_devices + q % rep_devices))
    return found


def per_device(features, weight, tile_values, tile_rows, tile_cols, tile_count, train_mask, upstream):
    rows_n, reps = lax.axis_size("row"), lax.axis_size("rep")
    sections = rows_n // reps
    mine = lax.axis_index("rep").astype(jnp.int32).reshape(1)

    def moved(value, target):
        return lax.ppermute(value, ("row", "rep"), pairs(rows_n, reps, target))

    first = moved(features, lambda j, r: (j + sections * r, r))
    panels = build(tile_values[0, 0], tile_rows[0, 0], tile_cols[0, 0], tile_count[0, 0])
    second = moved(first, lambda i, r: (i - 1, r - 1) if i % 2 else (i + 1, r))
    cotangent = upstream.astype(jnp.float32) * train_mask.astype(jnp.float32)[:, None]

    partial_rows = forward(mine, panels, first, second, reps)
    received = [partial_rows[0]] + [
        moved(partial_rows[d], lambda i, r, d=d: (i, r + d)) for d in range(1, reps)
    ]
    activated, back, term, sends = middle(mine, received, weight, cotangent)

    arrived = [moved(send, lambda i, r, d=d: (i, r + d)) for d, send in enumerate(sends, 1)]
    backs = [back] + arrived
    late = backward(1, False, mine, panels, backs, jnp.bfloat16)
    late = moved(late, lambda i, r: (i - 1, r) if i % 2 else (i + 1, r + 1))
    early = backward(0, True, mine, panels, backs, jnp.float32)
    merged = merge(mine, early, late)
    homes = [
        moved(piece, lambda i, r, d=d: (i - sections * r, r + d)) for d, piece in enumerate(merged)
    ]
    feature_grad = finish(homes)

    width = weight.shape[0]
    some = width // reps
    strip = lax.dynamic_slice_in_dim(term, mine[0] * some, some, 0)
    for piece in arrived:
        strip = strip + piece[width:].astype(jnp.float32)
    bit = 1
    while bit < rows_n:
        strip = strip + moved(strip, lambda i, r, bit=bit: (i ^ bit, r))
        bit *= 2
    scale = 1.0 / math.sqrt(features.shape[0] * rows_n)
    whole = strip * scale
    bit = 1
    while bit < reps:
        other = moved(whole, lambda i, r, bit=bit: (i, r ^ bit))
        upper = (mine[0] & bit) != 0
        whole = jnp.where(upper, jnp.concatenate([other, whole], 0), jnp.concatenate([whole, other], 0))
        bit *= 2
    return activated, whole, feature_grad


def solution(mesh):
    placed = (
        P("row", None),
        P(),
        P("row", "rep", None, None, None, None),
        P("row", "rep", None, None),
        P("row", "rep", None, None),
        P("row", "rep", None),
        P(("row", "rep")),
        P(("row", "rep"), None),
    )
    return jax.shard_map(
        per_device,
        mesh=mesh,
        in_specs=placed,
        out_specs=(P(("row", "rep"), None), P(), P(("row", "rep"), None)),
        check_vma=False,
    )
```

time: 676 us -> 178 us (0.26)
  waiting for transfers between devices: 462 us -> 56.4 us
  other arithmetic: 101 us -> 0.9 us
  starting transfers between devices: 7.95 us -> 80.1 us
  local copies, waits for them, and re-layouts: 63.5 us -> 23.9 us
  matrix products: 25.1 us -> 0 us
  Pallas kernels: 0 us -> 16.8 us
  between operations: 14 us -> 0.81 us
    psum x3 -> x0, waiting for transfers between devices: 275 us -> none  [the longest x1 123 us: per_device(): lax.psum(local_term, ('row', 'rep'))]
    ppermute x9 -> x32, waiting for transfers between devices: 161 us -> 56.4 us  [moved(): return lax.ppermute(value, ('row', 'rep'), pairs(rows_n, reps, target))]
    scatter-add x2 -> x0, other arithmetic: 80 us -> none  [dense_block(): return empty.at[row_index, col_index].add(zeroed)]
    ppermute x9 -> x32, starting transfers between devices: 7.78 us -> 80.1 us  [moved(): return lax.ppermute(value, ('row', 'rep'), pairs(rows_n, reps, target))]
    dot_general x4 -> x0, local copies, waits for them, and re-layouts: 52.2 us -> none  [the longest x2 27.4 us: dense_apply(): jnp.einsum('abij,bjf->aif', dense, pieces, preferred_element_type=jnp.flo...]
    all_gather x1 -> x0, waiting for transfers between devices: 25.8 us -> none  [per_device(): back_block = lax.all_gather(back_share, 'rep', axis=0, tiled=True)]
    dot_general x7 -> x0, matrix products: 25.1 us -> none  [the longest x2 10.8 us: dense_apply(): jnp.einsum('abij,aif->bjf', dense, pieces, preferred_element_type=jnp.flo...]
    unnamed x16 -> x20, local copies, waits for them, and re-layouts: 0.04 us -> 23.9 us
  transfers between devices with their start and end apart: 13 -> 32, of which waited for: 12 -> 14; matrix products, arithmetic and copies ran while one was open for 24% -> 1% of each run, Pallas kernels for 0% -> 5%
where the time goes in v1:
time: 178 us; the launch traced here: 179 us
  starting transfers between devices  80.1 us (45%)
  waiting for transfers between devices  56.4 us (32%)
  local copies, waits for them, and re-layouts  23.9 us (13%)
  Pallas kernels  16.8 us (9%)
    ppermute x32, starting transfers between devices, moved(): return lax.ppermute(value, ('row', 'rep'), pairs(rows_n, reps, target))  80.1 us
    ppermute x32, waiting for transfers between devices, moved(): return lax.ppermute(value, ('row', 'rep'), pairs(rows_n, reps, target))  56.4 us
    unnamed x20, local copies, waits for them, and re-layouts  23.9 us
    pallas_call x1, Pallas kernels, build(): pl.pallas_call(build_kernel, grid_spec=pltpu.PrefetchScalarGridSpec(num_s...  5.6 us
    pallas_call x2, Pallas kernels, backward(): pl.pallas_call(functools.partial(backward_kernel, part, share, rotate), i...  4.65 us
    pallas_call x1, Pallas kernels, forward(): pl.pallas_call(functools.partial(forward_kernel, share), in_specs=[SMEM,...  4.49 us
  transfers between devices with their start and end apart: 32, of which 14 were waited for; matrix products, arithmetic and copies ran while one was open for 1% of the time, Pallas kernels for 5%

profile of v1, /device:TPU:8, one launch (start us, length us, event | category | flops | bytes accessed | tf_op | source)
XLA Modules:
  0.0 178.9 jit_solution(17016597352313822658)
XLA Ops:
  0.6 5.8 %collective-permute-start = (bf16[2048,256]{1,0:T(8,128)(2,1)}, bf16[2048,256]{1,0:T(8,128)(2,1)S(1)}, u32[]{:S(2)}, u32[]{:S(2)}) collective-permute-start(bf16[2048,256]{1,0:T(8,128)(2,1)} %param.8), channel_id=1, source_target_pairs={{0,0},{1,17},{2,34},{3,51},{4,68},{5,85},{6,102},{7,119},{8,8},{9,... | collective-permute-start | bytes 3145736 | tf_op jit(solution)/shard_map/ppermute | solution.py:224
  6.4 25.5 %collective-permute-done.first = bf16[2048,256]{1,0:T(8,128)(2,1)S(1)} collective-permute-done((bf16[2048,256]{1,0:T(8,128)(2,1)}, bf16[2048,256]{1,0:T(8,128)(2,1)S(1)}, u32[]{:S(2)}, u32[]{:S(2)}) %collective-permute-start) | collective-permute-done | bytes 1048608 | tf_op jit(solution)/shard_map/ppermute | solution.py:224
  32.0 4.6 %copy-done.3 = bf16[1,1,2,192,128,128]{5,4,3,2,1,0:T(8,128)(2,1)S(1)} copy-done((bf16[1,1,2,192,128,128]{5,4,3,2,1,0:T(8,128)(2,1)S(1)}, bf16[1,1,2,192,128,128]{5,4,3,2,1,0:T(8,128)(2,1)}, u32[]{:S(2)}) %copy-start.3) | copy-done | bytes 12582936
  38.6 5.6 %build.1.panels = bf16[2,16,2048,128]{3,2,1,0:T(8,128)(2,1)S(1)} custom-call(s32[2,192]{1,0:T(2,128)S(1)} %bitcast.6, s32[2,192]{1,0:T(2,128)S(1)} %bitcast.7, s32[2]{0:T(128)S(1)} %bitcast.8, bf16[2,192,128,128]{3,2,1,0:T(8,128)(2,1)S(1)} %bitcast.5), custom_call_target="tpu_custom_call" | custom-call | bytes 31457280 | tf_op jit(solution)/shard_map/build/pallas_call | solution.py:55
  46.2 4.5 %forward.1 = (bf16[256,256]{1,0:T(8,128)(2,1)S(1)}, bf16[256,256]{1,0:T(8,128)(2,1)S(1)}, bf16[256,256]{1,0:T(8,128)(2,1)S(1)}, bf16[256,256]{1,0:T(8,128)(2,1)S...) custom-call(s32[1]{0:T(128)} %bitcast.mine, ...), custom_call_target="tpu_custom_call" | custom-call | flops 4294967296 | bytes 4194304 | tf_op jit(solution)/shard_map/forward/pallas_call | solution.py:86
  50.7 5.8 %copy-done = bf16[2,16,2048,128]{3,2,1,0:T(8,128)(2,1)} copy-done((bf16[2,16,2048,128]{3,2,1,0:T(8,128)(2,1)}, bf16[2,16,2048,128]{3,2,1,0:T(8,128)(2,1)S(1)}, u32[]{:S(2)}) %copy-start) | copy-done | bytes 16777240
  56.7 4.4 %collective-permute-start.3 = (bf16[256,256]{1,0:T(8,128)(2,1)S(1)}, bf16[256,256]{1,0:T(8,128)(2,1)S(1)}, u32[]{:S(2)}, u32[]{:S(2)}) collective-permute-start(bf16[256,256]{1,0:T(8,128)(2,1)S(1)} %get-tuple-element.31), channel_id=1, source_target_pairs={{0,2},{1,3},{2,4},{3,5},{4,6},{5,7},{6,0},{7,1},{8,10},{9,11},{10,... | collective-permute-start | bytes 393224 | tf_op jit(solution)/shard_map/ppermute | solution.py:224
  69.9 3.9 %collective-permute-done.5.refs_4_ = bf16[256,256]{1,0:T(8,128)(2,1)S(1)} collective-permute-done((bf16[256,256]{1,0:T(8,128)(2,1)S(1)}, bf16[256,256]{1,0:T(8,128)(2,1)S(1)}, u32[]{:S(2)}, u32[]{:S(2)}) %collective-permute-start.5) | collective-permute-done | bytes 131104 | tf_op jit(solution)/shard_map/ppermute | solution.py:224
  80.3 2.8 %collective-permute-start.11 = (bf16[288,256]{1,0:T(8,128)(2,1)S(1)}, bf16[288,256]{1,0:T(8,128)(2,1)S(1)}, u32[]{:S(2)}, u32[]{:S(2)}) collective-permute-start(bf16[288,256]{1,0:T(8,128)(2,1)S(1)} %get-tuple-element.41), channel_id=1, source_target_pairs={{0,3},{1,4},{2,5},{3,6},{4,7},{5,0},{6,1},{7,2},{8,11},{9,12},{10,... | collective-permute-start | bytes 442376 | tf_op jit(solution)/shard_map/ppermute | solution.py:224
  84.2 2.9 %collective-permute-start.14 = (bf16[288,256]{1,0:T(8,128)(2,1)S(1)}, bf16[288,256]{1,0:T(8,128)(2,1)S(1)}, u32[]{:S(2)}, u32[]{:S(2)}) collective-permute-start(bf16[288,256]{1,0:T(8,128)(2,1)S(1)} %get-tuple-element.44), channel_id=1, source_target_pairs={{0,6},{1,7},{2,0},{3,1},{4,2},{5,3},{6,4},{7,5},{8,14},{9,15},{10,... | collective-permute-start | bytes 442376 | tf_op jit(solution)/shard_map/ppermute | solution.py:224
  88.0 4.0 %collective-permute-start.15 = (bf16[288,256]{1,0:T(8,128)(2,1)S(1)}, bf16[288,256]{1,0:T(8,128)(2,1)S(1)}, u32[]{:S(2)}, u32[]{:S(2)}) collective-permute-start(bf16[288,256]{1,0:T(8,128)(2,1)S(1)} %get-tuple-element.45), channel_id=1, source_target_pairs={{0,7},{1,0},{2,1},{3,2},{4,3},{5,4},{6,5},{7,6},{8,15},{9,8},{10,9... | collective-permute-start | bytes 442376 | tf_op jit(solution)/shard_map/ppermute | solution.py:224
  92.1 2.6 %collective-permute-done.12.refs_4_ = bf16[288,256]{1,0:T(8,128)(2,1)S(1)} collective-permute-done((bf16[288,256]{1,0:T(8,128)(2,1)S(1)}, bf16[288,256]{1,0:T(8,128)(2,1)S(1)}, u32[]{:S(2)}, u32[]{:S(2)}) %collective-permute-start.12) | collective-permute-done | bytes 147488 | tf_op jit(solution)/shard_map/ppermute | solution.py:224
  95.9 5.8 %copy-done.1 = bf16[2,16,2048,128]{3,2,1,0:T(8,128)(2,1)S(1)} copy-done((bf16[2,16,2048,128]{3,2,1,0:T(8,128)(2,1)S(1)}, bf16[2,16,2048,128]{3,2,1,0:T(8,128)(2,1)}, u32[]{:S(2)}) %copy-start.1) | copy-done | bytes 16777240
  107.3 4.9 %collective-permute-done.17 = f32[32,256]{1,0:T(8,128)S(1)} collective-permute-done((f32[32,256]{1,0:T(8,128)S(1)}, f32[32,256]{1,0:T(8,128)S(1)}, u32[]{:S(2)}, u32[]{:S(2)}) %collective-permute-start.17) | collective-permute-done | bytes 32800 | tf_op jit(solution)/shard_map/ppermute | solution.py:224
  112.8 3.4 %collective-permute-done.18 = f32[32,256]{1,0:T(8,128)S(1)} collective-permute-done((f32[32,256]{1,0:T(8,128)S(1)}, f32[32,256]{1,0:T(8,128)S(1)}, u32[]{:S(2)}, u32[]{:S(2)}) %collective-permute-start.18) | collective-permute-done | bytes 32800 | tf_op jit(solution)/shard_map/ppermute | solution.py:224
  116.1 3.6 %collective-permute-start.19 = (f32[32,256]{1,0:T(8,128)S(1)}, f32[32,256]{1,0:T(8,128)S(1)}, u32[]{:S(2)}, u32[]{:S(2)}) collective-permute-start(f32[32,256]{1,0:T(8,128)S(1)} %add.46), channel_id=1, source_target_pairs={{0,64},{1,65},{2,66},{3,67},{4,68},{5,69},{6,70},{7,71},{8,72},{9,... | collective-permute-start | bytes 98312 | tf_op jit(solution)/shard_map/ppermute | solution.py:224
  121.7 11.2 %collective-permute-start.20 = (f32[32,256]{1,0:T(8,128)S(1)}, f32[32,256]{1,0:T(8,128)S(1)}, u32[]{:S(2)}, u32[]{:S(2)}) collective-permute-start(f32[32,256]{1,0:T(8,128)S(1)} %add_multiply_fusion), channel_id=1, source_target_pairs={{0,1},{1,0},{2,3},{3,2},{4,5},{5,4},{6,7},{7,6},{8,9},{9,8},{10,11... | collective-permute-start | bytes 98312 | tf_op jit(solution)/shard_map/ppermute | solution.py:224
  134.8 5.8 %copy-done.2 = bf16[2,16,2048,128]{3,2,1,0:T(8,128)(2,1)S(1)} copy-done((bf16[2,16,2048,128]{3,2,1,0:T(8,128)(2,1)S(1)}, bf16[2,16,2048,128]{3,2,1,0:T(8,128)(2,1)}, u32[]{:S(2)}) %copy-start.2) | copy-done | bytes 16777240
  143.8 6.0 %collective-permute-start.24 = (bf16[256,256]{1,0:T(8,128)(2,1)S(1)}, bf16[256,256]{1,0:T(8,128)(2,1)S(1)}, u32[]{:S(2)}, u32[]{:S(2)}) collective-permute-start(bf16[256,256]{1,0:T(8,128)(2,1)S(1)} %get-tuple-element.47), channel_id=1, source_target_pairs={{0,0},{1,113},{2,98},{3,83},{4,68},{5,53},{6,38},{7,23},{8,8},{9,1... | collective-permute-start | bytes 393224 | tf_op jit(solution)/shard_map/ppermute | solution.py:224
  149.8 2.6 %collective-permute-start.25 = (bf16[256,256]{1,0:T(8,128)(2,1)S(1)}, bf16[256,256]{1,0:T(8,128)(2,1)S(1)}, u32[]{:S(2)}, u32[]{:S(2)}) collective-permute-start(bf16[256,256]{1,0:T(8,128)(2,1)S(1)} %get-tuple-element.48), channel_id=1, source_target_pairs={{0,1},{1,114},{2,99},{3,84},{4,69},{5,54},{6,39},{7,16},{8,9},{9,1... | collective-permute-start | bytes 393224 | tf_op jit(solution)/shard_map/ppermute | solution.py:224
  152.4 3.0 %collective-permute-start.26 = (bf16[256,256]{1,0:T(8,128)(2,1)S(1)}, bf16[256,256]{1,0:T(8,128)(2,1)S(1)}, u32[]{:S(2)}, u32[]{:S(2)}) collective-permute-start(bf16[256,256]{1,0:T(8,128)(2,1)S(1)} %get-tuple-element.49), channel_id=1, source_target_pairs={{0,2},{1,115},{2,100},{3,85},{4,70},{5,55},{6,32},{7,17},{8,10},{9... | collective-permute-start | bytes 393224 | tf_op jit(solution)/shard_map/ppermute | solution.py:224
  155.4 6.4 %collective-permute-start.27 = (bf16[256,256]{1,0:T(8,128)(2,1)S(1)}, bf16[256,256]{1,0:T(8,128)(2,1)S(1)}, u32[]{:S(2)}, u32[]{:S(2)}) collective-permute-start(bf16[256,256]{1,0:T(8,128)(2,1)S(1)} %get-tuple-element.50), channel_id=1, source_target_pairs={{0,3},{1,116},{2,101},{3,86},{4,71},{5,48},{6,33},{7,18},{8,11},{9... | collective-permute-start | bytes 393224 | tf_op jit(solution)/shard_map/ppermute | solution.py:224
  163.0 9.2 %collective-permute-start.30 = (bf16[256,256]{1,0:T(8,128)(2,1)S(1)}, bf16[256,256]{1,0:T(8,128)(2,1)S(1)}, u32[]{:S(2)}, u32[]{:S(2)}) collective-permute-start(bf16[256,256]{1,0:T(8,128)(2,1)S(1)} %get-tuple-element.53), channel_id=1, source_target_pairs={{0,6},{1,119},{2,96},{3,81},{4,66},{5,51},{6,36},{7,21},{8,14},{9,... | collective-permute-start | bytes 393224 | tf_op jit(solution)/shard_map/ppermute | solution.py:224
  174.7 3.3 %collective-permute-done.31.refs_7_ = bf16[256,256]{1,0:T(8,128)(2,1)S(1)} collective-permute-done((bf16[256,256]{1,0:T(8,128)(2,1)S(1)}, bf16[256,256]{1,0:T(8,128)(2,1)S(1)}, u32[]{:S(2)}, u32[]{:S(2)}) %collective-permute-start.31) | collective-permute-done | bytes 131104 | tf_op jit(solution)/shard_map/ppermute | solution.py:224
  (77 shorter events, 40.6 us)
Async XLA Ops:
  0.6 31.3 %collective-permute-start = (bf16[2048,256]{1,0:T(8,128)(2,1)}, bf16[2048,256]{1,0:T(8,128)(2,1)S(1)}, u32[]{:S(2)}, u32[]{:S(2)}) collective-permute-start(bf16[2048,256]{1,0:T(8,128)(2,1)} %param.8), channel_id=1, source_target_pairs={{0,0},{1,17},{2,34},{3,51},{4,68},{5,85},{6,102},{7,119},{8,8},{9,... | collective-permute-start | bytes 3145736 | tf_op jit(solution)/shard_map/ppermute | solution.py:224
  32.0 14.2 %collective-permute-start.1 = (bf16[2048,256]{1,0:T(8,128)(2,1)S(1)}, bf16[2048,256]{1,0:T(8,128)(2,1)S(1)}, u32[]{:S(2)}, u32[]{:S(2)}) collective-permute-start(bf16[2048,256]{1,0:T(8,128)(2,1)S(1)} %collective-permute-done.first), channel_id=1, source_target_pairs={{0,8},{1,9},{2,10},{3,11},{4,12},{5,13},{6,14},{7,15},{8,7},{9,0},... | collective-permute-start | bytes 3145736 | tf_op jit(solution)/shard_map/ppermute | solution.py:224
  56.5 8.8 %collective-permute-start.2 = (bf16[256,256]{1,0:T(8,128)(2,1)S(1)}, bf16[256,256]{1,0:T(8,128)(2,1)S(1)}, u32[]{:S(2)}, u32[]{:S(2)}) collective-permute-start(bf16[256,256]{1,0:T(8,128)(2,1)S(1)} %get-tuple-element.30), channel_id=1, source_target_pairs={{0,1},{1,2},{2,3},{3,4},{4,5},{5,6},{6,7},{7,0},{8,9},{9,10},{10,1... | collective-permute-start | bytes 393224 | tf_op jit(solution)/shard_map/ppermute | solution.py:224
  56.7 10.7 %collective-permute-start.3 = (bf16[256,256]{1,0:T(8,128)(2,1)S(1)}, bf16[256,256]{1,0:T(8,128)(2,1)S(1)}, u32[]{:S(2)}, u32[]{:S(2)}) collective-permute-start(bf16[256,256]{1,0:T(8,128)(2,1)S(1)} %get-tuple-element.31), channel_id=1, source_target_pairs={{0,2},{1,3},{2,4},{3,5},{4,6},{5,7},{6,0},{7,1},{8,10},{9,11},{10,... | collective-permute-start | bytes 393224 | tf_op jit(solution)/shard_map/ppermute | solution.py:224
  61.1 8.7 %collective-permute-start.4 = (bf16[256,256]{1,0:T(8,128)(2,1)S(1)}, bf16[256,256]{1,0:T(8,128)(2,1)S(1)}, u32[]{:S(2)}, u32[]{:S(2)}) collective-permute-start(bf16[256,256]{1,0:T(8,128)(2,1)S(1)} %get-tuple-element.32), channel_id=1, source_target_pairs={{0,3},{1,4},{2,5},{3,6},{4,7},{5,0},{6,1},{7,2},{8,11},{9,12},{10,... | collective-permute-start | bytes 393224 | tf_op jit(solution)/shard_map/ppermute | solution.py:224
  63.3 10.5 %collective-permute-start.5 = (bf16[256,256]{1,0:T(8,128)(2,1)S(1)}, bf16[256,256]{1,0:T(8,128)(2,1)S(1)}, u32[]{:S(2)}, u32[]{:S(2)}) collective-permute-start(bf16[256,256]{1,0:T(8,128)(2,1)S(1)} %get-tuple-element.33), channel_id=1, source_target_pairs={{0,4},{1,5},{2,6},{3,7},{4,0},{5,1},{6,2},{7,3},{8,12},{9,13},{10,... | collective-permute-start | bytes 393224 | tf_op jit(solution)/shard_map/ppermute | solution.py:224
  65.2 8.6 %collective-permute-start.6 = (bf16[256,256]{1,0:T(8,128)(2,1)S(1)}, bf16[256,256]{1,0:T(8,128)(2,1)S(1)}, u32[]{:S(2)}, u32[]{:S(2)}) collective-permute-start(bf16[256,256]{1,0:T(8,128)(2,1)S(1)} %get-tuple-element.34), channel_id=1, source_target_pairs={{0,5},{1,6},{2,7},{3,0},{4,1},{5,2},{6,3},{7,4},{8,13},{9,14},{10,... | collective-permute-start | bytes 393224 | tf_op jit(solution)/shard_map/ppermute | solution.py:224
  65.2 8.6 %collective-permute-start.7 = (bf16[256,256]{1,0:T(8,128)(2,1)S(1)}, bf16[256,256]{1,0:T(8,128)(2,1)S(1)}, u32[]{:S(2)}, u32[]{:S(2)}) collective-permute-start(bf16[256,256]{1,0:T(8,128)(2,1)S(1)} %get-tuple-element.35), channel_id=1, source_target_pairs={{0,6},{1,7},{2,0},{3,1},{4,2},{5,3},{6,4},{7,5},{8,14},{9,15},{10,... | collective-permute-start | bytes 393224 | tf_op jit(solution)/shard_map/ppermute | solution.py:224
  75.7 8.5 %collective-permute-start.9 = (bf16[288,256]{1,0:T(8,128)(2,1)S(1)}, bf16[288,256]{1,0:T(8,128)(2,1)S(1)}, u32[]{:S(2)}, u32[]{:S(2)}) collective-permute-start(bf16[288,256]{1,0:T(8,128)(2,1)S(1)} %get-tuple-element.39), channel_id=1, source_target_pairs={{0,1},{1,2},{2,3},{3,4},{4,5},{5,6},{6,7},{7,0},{8,9},{9,10},{10,1... | collective-permute-start | bytes 442376 | tf_op jit(solution)/shard_map/ppermute | solution.py:224
  78.0 10.0 %collective-permute-start.10 = (bf16[288,256]{1,0:T(8,128)(2,1)S(1)}, bf16[288,256]{1,0:T(8,128)(2,1)S(1)}, u32[]{:S(2)}, u32[]{:S(2)}) collective-permute-start(bf16[288,256]{1,0:T(8,128)(2,1)S(1)} %get-tuple-element.40), channel_id=1, source_target_pairs={{0,2},{1,3},{2,4},{3,5},{4,6},{5,7},{6,0},{7,1},{8,10},{9,11},{10,... | collective-permute-start | bytes 442376 | tf_op jit(solution)/shard_map/ppermute | solution.py:224
  80.3 11.7 %collective-permute-start.11 = (bf16[288,256]{1,0:T(8,128)(2,1)S(1)}, bf16[288,256]{1,0:T(8,128)(2,1)S(1)}, u32[]{:S(2)}, u32[]{:S(2)}) collective-permute-start(bf16[288,256]{1,0:T(8,128)(2,1)S(1)} %get-tuple-element.41), channel_id=1, source_target_pairs={{0,3},{1,4},{2,5},{3,6},{4,7},{5,0},{6,1},{7,2},{8,11},{9,12},{10,... | collective-permute-start | bytes 442376 | tf_op jit(solution)/shard_map/ppermute | solution.py:224
  83.1 11.5 %collective-permute-start.12 = (bf16[288,256]{1,0:T(8,128)(2,1)S(1)}, bf16[288,256]{1,0:T(8,128)(2,1)S(1)}, u32[]{:S(2)}, u32[]{:S(2)}) collective-permute-start(bf16[288,256]{1,0:T(8,128)(2,1)S(1)} %get-tuple-element.42), channel_id=1, source_target_pairs={{0,4},{1,5},{2,6},{3,7},{4,0},{5,1},{6,2},{7,3},{8,12},{9,13},{10,... | collective-permute-start | bytes 442376 | tf_op jit(solution)/shard_map/ppermute | solution.py:224
  83.1 11.5 %collective-permute-start.13 = (bf16[288,256]{1,0:T(8,128)(2,1)S(1)}, bf16[288,256]{1,0:T(8,128)(2,1)S(1)}, u32[]{:S(2)}, u32[]{:S(2)}) collective-permute-start(bf16[288,256]{1,0:T(8,128)(2,1)S(1)} %get-tuple-element.43), channel_id=1, source_target_pairs={{0,5},{1,6},{2,7},{3,0},{4,1},{5,2},{6,3},{7,4},{8,13},{9,14},{10,... | collective-permute-start | bytes 442376 | tf_op jit(solution)/shard_map/ppermute | solution.py:224
  84.2 10.4 %collective-permute-start.14 = (bf16[288,256]{1,0:T(8,128)(2,1)S(1)}, bf16[288,256]{1,0:T(8,128)(2,1)S(1)}, u32[]{:S(2)}, u32[]{:S(2)}) collective-permute-start(bf16[288,256]{1,0:T(8,128)(2,1)S(1)} %get-tuple-element.44), channel_id=1, source_target_pairs={{0,6},{1,7},{2,0},{3,1},{4,2},{5,3},{6,4},{7,5},{8,14},{9,15},{10,... | collective-permute-start | bytes 442376 | tf_op jit(solution)/shard_map/ppermute | solution.py:224
  104.0 39.5 %collective-permute-start.23 = (bf16[8,256,256]{2,1,0:T(8,128)(2,1)S(1)}, bf16[8,256,256]{2,1,0:T(8,128)(2,1)S(1)}, u32[]{:S(2)}, u32[]{:S(2)}) collective-permute-start(bf16[8,256,256]{2,1,0:T(8,128)(2,1)S(1)} %backward.3), channel_id=1, source_target_pairs={{0,9},{1,10},{2,11},{3,12},{4,13},{5,14},{6,15},{7,8},{8,0},{9,1},... | collective-permute-start | bytes 3145736 | tf_op jit(solution)/shard_map/ppermute | solution.py:224
  121.7 13.1 %collective-permute-start.20 = (f32[32,256]{1,0:T(8,128)S(1)}, f32[32,256]{1,0:T(8,128)S(1)}, u32[]{:S(2)}, u32[]{:S(2)}) collective-permute-start(f32[32,256]{1,0:T(8,128)S(1)} %add_multiply_fusion), channel_id=1, source_target_pairs={{0,1},{1,0},{2,3},{3,2},{4,5},{5,4},{6,7},{7,6},{8,9},{9,8},{10,11... | collective-permute-start | bytes 98312 | tf_op jit(solution)/shard_map/ppermute | solution.py:224
  143.0 18.9 %collective-permute-start.22 = (f32[128,256]{1,0:T(8,128)S(1)}, f32[128,256]{1,0:T(8,128)S(1)}, u32[]{:S(2)}, u32[]{:S(2)}) collective-permute-start(f32[128,256]{1,0:T(8,128)S(1)} %maximum_select_fusion.1), channel_id=1, source_target_pairs={{0,4},{1,5},{2,6},{3,7},{4,0},{5,1},{6,2},{7,3},{8,12},{9,13},{10,... | collective-permute-start | bytes 393224 | tf_op jit(solution)/shard_map/ppermute | solution.py:224
  143.8 18.1 %collective-permute-start.24 = (bf16[256,256]{1,0:T(8,128)(2,1)S(1)}, bf16[256,256]{1,0:T(8,128)(2,1)S(1)}, u32[]{:S(2)}, u32[]{:S(2)}) collective-permute-start(bf16[256,256]{1,0:T(8,128)(2,1)S(1)} %get-tuple-element.47), channel_id=1, source_target_pairs={{0,0},{1,113},{2,98},{3,83},{4,68},{5,53},{6,38},{7,23},{8,8},{9,1... | collective-permute-start | bytes 393224 | tf_op jit(solution)/shard_map/ppermute | solution.py:224
  149.8 13.2 %collective-permute-start.25 = (bf16[256,256]{1,0:T(8,128)(2,1)S(1)}, bf16[256,256]{1,0:T(8,128)(2,1)S(1)}, u32[]{:S(2)}, u32[]{:S(2)}) collective-permute-start(bf16[256,256]{1,0:T(8,128)(2,1)S(1)} %get-tuple-element.48), channel_id=1, source_target_pairs={{0,1},{1,114},{2,99},{3,84},{4,69},{5,54},{6,39},{7,16},{8,9},{9,1... | collective-permute-start | bytes 393224 | tf_op jit(solution)/shard_map/ppermute | solution.py:224
  152.4 19.8 %collective-permute-start.26 = (bf16[256,256]{1,0:T(8,128)(2,1)S(1)}, bf16[256,256]{1,0:T(8,128)(2,1)S(1)}, u32[]{:S(2)}, u32[]{:S(2)}) collective-permute-start(bf16[256,256]{1,0:T(8,128)(2,1)S(1)} %get-tuple-element.49), channel_id=1, source_target_pairs={{0,2},{1,115},{2,100},{3,85},{4,70},{5,55},{6,32},{7,17},{8,10},{9... | collective-permute-start | bytes 393224 | tf_op jit(solution)/shard_map/ppermute | solution.py:224
  155.4 17.5 %collective-permute-start.27 = (bf16[256,256]{1,0:T(8,128)(2,1)S(1)}, bf16[256,256]{1,0:T(8,128)(2,1)S(1)}, u32[]{:S(2)}, u32[]{:S(2)}) collective-permute-start(bf16[256,256]{1,0:T(8,128)(2,1)S(1)} %get-tuple-element.50), channel_id=1, source_target_pairs={{0,3},{1,116},{2,101},{3,86},{4,71},{5,48},{6,33},{7,18},{8,11},{9... | collective-permute-start | bytes 393224 | tf_op jit(solution)/shard_map/ppermute | solution.py:224
  161.9 11.1 %collective-permute-start.28 = (bf16[256,256]{1,0:T(8,128)(2,1)S(1)}, bf16[256,256]{1,0:T(8,128)(2,1)S(1)}, u32[]{:S(2)}, u32[]{:S(2)}) collective-permute-start(bf16[256,256]{1,0:T(8,128)(2,1)S(1)} %get-tuple-element.51), channel_id=1, source_target_pairs={{0,4},{1,117},{2,102},{3,87},{4,64},{5,49},{6,34},{7,19},{8,12},{9... | collective-permute-start | bytes 393224 | tf_op jit(solution)/shard_map/ppermute | solution.py:224
  161.9 11.1 %collective-permute-start.29 = (bf16[256,256]{1,0:T(8,128)(2,1)S(1)}, bf16[256,256]{1,0:T(8,128)(2,1)S(1)}, u32[]{:S(2)}, u32[]{:S(2)}) collective-permute-start(bf16[256,256]{1,0:T(8,128)(2,1)S(1)} %get-tuple-element.52), channel_id=1, source_target_pairs={{0,5},{1,118},{2,103},{3,80},{4,65},{5,50},{6,35},{7,20},{8,13},{9... | collective-permute-start | bytes 393224 | tf_op jit(solution)/shard_map/ppermute | solution.py:224
  163.0 11.7 %collective-permute-start.30 = (bf16[256,256]{1,0:T(8,128)(2,1)S(1)}, bf16[256,256]{1,0:T(8,128)(2,1)S(1)}, u32[]{:S(2)}, u32[]{:S(2)}) collective-permute-start(bf16[256,256]{1,0:T(8,128)(2,1)S(1)} %get-tuple-element.53), channel_id=1, source_target_pairs={{0,6},{1,119},{2,96},{3,81},{4,66},{5,51},{6,36},{7,21},{8,14},{9,... | collective-permute-start | bytes 393224 | tf_op jit(solution)/shard_map/ppermute | solution.py:224
  (18 other events, 143.5 us)

commit v2 on v1

v2 whole, which is shorter than its diff:
```python
import functools
import math

import jax
import jax.numpy as jnp
from jax import lax
from jax.experimental import pallas as pl
from jax.experimental.pallas import tpu as pltpu
from jax.sharding import PartitionSpec as P

TB = 16
TILE = 128
CHUNK = 48
VMEM = pl.BlockSpec(memory_space=pltpu.VMEM)
SMEM = pl.BlockSpec(memory_space=pltpu.SMEM)
NT = (((1,), (1,)), ((), ()))
TN = (((0,), (0,)), ((), ()))


def params(mib, **more):
    return pltpu.CompilerParams(vmem_limit_bytes=mib << 20, **more)


def in_vmem(array):
    return pltpu.with_memory_space_constraint(array, pltpu.VMEM)


def build_kernel(part, rows, cols, count, tiles, *refs):
    panels, token = refs[-2:]
    chunk = pl.program_id(0)
    token[...] = jnp.zeros(token.shape, token.dtype)

    @pl.when(chunk == 0)
    def _():
        def clear(b, carry):
            panels[part, b] = jnp.zeros(panels.shape[2:], panels.dtype)
            return carry

        lax.fori_loop(0, TB, clear, 0)

    def place(t, carry):
        slot = chunk * CHUNK + t
        row = pl.multiple_of(rows[part, slot] * TILE, TILE)
        panels[part, cols[part, slot], pl.ds(row, TILE), :] = tiles[0, t]
        return carry

    lax.fori_loop(0, jnp.clip(count[part] - chunk * CHUNK, 0, CHUNK), place, 0)


def build(part, tile_values, tile_rows, tile_cols, tile_count, *more):
    sections, slots = tile_rows.shape

    def block(chunk, rows, cols, count):
        last = lax.div(count[part] - 1, CHUNK)
        return part, jnp.minimum(chunk, last), 0, 0

    return pl.pallas_call(
        functools.partial(build_kernel, part),
        grid_spec=pltpu.PrefetchScalarGridSpec(
            num_scalar_prefetch=3,
            grid=(slots // CHUNK,),
            in_specs=[pl.BlockSpec((1, CHUNK, TILE, TILE), block)] + [VMEM] * len(more),
            out_specs=[VMEM, VMEM],
        ),
        out_shape=[
            pltpu.VMEM((sections, TB, TB * TILE, TILE), jnp.bfloat16),
            jax.ShapeDtypeStruct((8, 128), jnp.int32),
        ],
        input_output_aliases={4: 0} if more else {},
        compiler_params=params(12),
        cost_estimate=pl.CostEstimate(flops=0, bytes_accessed=15 << 20, transcendentals=0),
        name="build",
    )(tile_rows, tile_cols, tile_count, pltpu.with_memory_space_constraint(tile_values, pltpu.HBM), *map(in_vmem, more[:1]), *more[1:])


def place_of():
    return lax.axis_index("rep"), lax.rem(lax.axis_index("row"), 2)


def with_panels(kernel, name, panels, operands, outs, mib, flops=0):
    result = pl.pallas_call(
        kernel,
        in_specs=[VMEM] * (1 + len(operands)),
        out_specs=[VMEM] * (1 + len(outs)),
        out_shape=[pltpu.VMEM(panels.shape, panels.dtype), *outs],
        input_output_aliases={0: 0},
        compiler_params=params(mib),
        cost_estimate=pl.CostEstimate(flops=flops, bytes_accessed=2 << 20, transcendentals=0),
        name=name,
    )(in_vmem(panels), *operands)
    return result[0], result[1:]


def wide(panels, part, rows, at, size):
    return jnp.concatenate([panels[part, at + b, rows, :] for b in range(size)], axis=1)


def first_kernel(share, panels, source, token, same, out):
    replica, _ = place_of()
    for d in range(out.shape[0]):
        q = lax.rem(replica + d, out.shape[0])
        rows = pl.ds(pl.multiple_of(q * share, share), share)
        out[d] = jnp.dot(wide(panels, 0, rows, 0, TB), source[...], preferred_element_type=jnp.float32)


def second_kernel(share, shares, ds, panels, carried, inner, other, same, *outs):
    replica, core = place_of()
    source = jnp.where(core == 1, inner[...], other[...])
    for d, out in zip(ds, outs):
        q = lax.rem(replica + d, shares)
        rows = pl.ds(pl.multiple_of(q * share, share), share)
        total = carried[d] + jnp.dot(wide(panels, 1, rows, 0, TB), source, preferred_element_type=jnp.float32)
        out[...] = total.astype(out.dtype)


def middle_kernel(shares, panels, *refs):
    parts = refs[:shares]
    weight, upstream, train_mask, same, activated, back, term, *sends = refs[shares:]
    replica, _ = place_of()
    total = parts[0][...].astype(jnp.float32)
    for part in parts[1:]:
        total += part[...].astype(jnp.float32)
    aggregate = total.astype(jnp.bfloat16)
    logits = jnp.dot(aggregate, weight[...], preferred_element_type=jnp.float32)
    sigmoid_part = jax.nn.sigmoid(logits)
    activated[...] = (logits * sigmoid_part).astype(jnp.bfloat16)
    slope = sigmoid_part * (1.0 + logits * (1.0 - sigmoid_part))
    trained = jnp.broadcast_to(train_mask[...].astype(jnp.float32), logits.shape[::-1]).T
    masked = (upstream[...].astype(jnp.float32) * trained * slope).astype(jnp.bfloat16)
    turned = lax.dot_general(weight[...], masked, NT, preferred_element_type=jnp.float32).astype(jnp.bfloat16)
    back[...] = turned
    term[...] = lax.dot_general(aggregate, masked, TN, preferred_element_type=jnp.float32)
    width = weight.shape[0]
    some = width // shares
    for d, send in enumerate(sends, 1):
        at = pl.multiple_of(lax.rem(replica + d, shares) * some, some)
        send[:width, :] = turned
        send[width:, :] = term[pl.ds(at, some), :].astype(jnp.bfloat16)


def product_of(panels, part, q, es, backs, shares):
    replica, _ = place_of()
    width = share = backs[0].shape[1]
    total = None
    for e, back in zip(es, backs):
        p = lax.rem(replica + shares - e, shares)
        rows = pl.ds(pl.multiple_of(p * share, share), share)
        product = jnp.dot(back[:width, :], wide(panels, part, rows, 2 * q, 2), preferred_element_type=jnp.float32)
        total = product if total is None else total + product
    return total


def heads_kernel(shares, es, panels, *refs):
    backs = refs[: len(es)]
    same, late, early = refs[len(es) :]
    for part, out in ((1, late), (0, early)):
        for q in range(shares):
            out[q] = product_of(panels, part, q, es, backs, shares)


def tails_kernel(part, shares, es, qs, panels, carried, *refs):
    backs = refs[: len(es)]
    same, out = refs[len(es) :]
    for n, q in enumerate(qs):
        out[n] = (carried[q] + product_of(panels, part, q, es, backs, shares)).astype(out.dtype)


def tails_strip_kernel(part, shares, es, qs, panels, carried, *refs):
    backs, (term, *pieces) = refs[: len(es)], refs[len(es) : len(es) + 4]
    same, out, strips = refs[len(es) + 4 :]
    tails_kernel(part, shares, es, qs, panels, carried, *backs, same, out)
    replica, _ = place_of()
    width = term.shape[0]
    some = width // shares
    total = term[pl.ds(pl.multiple_of(replica * some, some), some), :]
    for piece in [*pieces, *backs]:
        total += piece[width:, :].astype(jnp.float32)
    for n in range(strips.shape[0]):
        strips[n] = total.astype(strips.dtype)


def merge_kernel(own, first, second, strips, *outs):
    replica, _ = place_of()
    half, width, _ = first.shape
    strip = strips[0].astype(jnp.float32)
    for n in range(1, strips.shape[0]):
        strip += strips[n].astype(jnp.float32)
    strip = strip.astype(jnp.bfloat16)
    for d, out in enumerate(outs):
        q = lax.rem(replica + d, len(outs))
        n = lax.rem(q, half)
        late = jnp.where(q < half, first[n], second[n])
        out[:width, :] = (own[q] + late.astype(jnp.float32)).astype(out.dtype)
        out[width:, :] = strip


def merge(own, first, second, strips):
    shares, width, share = own.shape
    return pl.pallas_call(
        merge_kernel,
        in_specs=[VMEM] * 4,
        out_specs=[VMEM] * shares,
        out_shape=[jax.ShapeDtypeStruct((width + strips.shape[1], share), jnp.bfloat16)] * shares,
        compiler_params=params(12),
        name="merge",
    )(own, first, second, strips)


def finish_kernel(scale, *refs):
    got, (home, whole) = refs[:-2], refs[-2:]
    replica, _ = place_of()
    width = whole.shape[0]
    some = width // len(got)
    total = got[0][:width, :].astype(jnp.float32)
    for part in got[1:]:
        total += part[:width, :].astype(jnp.float32)
    home[...] = total.T.astype(home.dtype)
    for d, part in enumerate(got):
        at = pl.multiple_of(lax.rem(replica + len(got) - d, len(got)) * some, some)
        whole[pl.ds(at, some), :] = part[width:, :].astype(jnp.float32) * scale


def finish(scale, width, got):
    share = got[0].shape[1]
    return pl.pallas_call(
        functools.partial(finish_kernel, scale),
        in_specs=[VMEM] * len(got),
        out_specs=[VMEM, VMEM],
        out_shape=[
            jax.ShapeDtypeStruct((share, width), jnp.bfloat16),
            jax.ShapeDtypeStruct((width, share), jnp.float32),
        ],
        compiler_params=params(12),
        name="finish",
    )(*got)


def pairs(row_devices, rep_devices, target):
    found = []
    for i in range(row_devices):
        for r in range(rep_devices):
            j, q = target(i, r)
            found.append((i * rep_devices + r, (j % row_devices) * rep_devices + q % rep_devices))
    return found


MAIN_FROM = (0, 5, 2, 4, 7, 1, 6, 3)
OTHER_FROM = (1, 6, 3, 0, 5, 2, 4, 7)


def per_device(features, weight, tile_values, tile_rows, tile_cols, tile_count, train_mask, upstream):
    rows_n, reps = lax.axis_size("row"), lax.axis_size("rep")
    sections = rows_n // reps
    width = weight.shape[0]
    share = features.shape[0] // reps
    bf16, f32 = jnp.bfloat16, jnp.float32

    def moved(value, target):
        return lax.ppermute(value, ("row", "rep"), pairs(rows_n, reps, target))

    def fetched(value, back, sources, wanted=lambda i: True):
        found = [
            (((i - sections * r - back) % rows_n) * reps + sources[r], i * reps + r)
            for i in range(rows_n)
            for r in range(reps)
            if wanted(i)
        ]
        return lax.ppermute(value, ("row", "rep"), found)

    def to_other_core(value):
        return lax.ppermute(value, ("row", "rep"), [((i - 1) * reps + r, i * reps + r) for i in range(1, rows_n, 2) for r in range(reps)])

    main = fetched(features, 0, MAIN_FROM)
    lists = tile_values[0, 0], tile_rows[0, 0], tile_cols[0, 0], tile_count[0, 0]
    panels, token = build(0, *lists)
    held, token = lax.optimization_barrier((features, token))
    other = fetched(held, 1, OTHER_FROM, lambda i: i % 2 == 0)
    panels, token = build(1, *lists, panels, token)
    main, token = lax.optimization_barrier((main, token))
    inner = to_other_core(main)

    flops = features.shape[0] ** 2 * 2 * width
    panels, (carried,) = with_panels(
        functools.partial(first_kernel, share), "first", panels, [main, token],
        [jax.ShapeDtypeStruct((reps, share, width), f32)], 12, flops,
    )
    shares_out = {}
    for ds in ((1, 2, 3, 4), (5, 6, 7, 0)):
        panels, outs = with_panels(
            functools.partial(second_kernel, share, reps, ds), "second", panels, [carried, inner, other],
            [jax.ShapeDtypeStruct((share, width), bf16)] * len(ds), 12, flops // 2,
        )
        shares_out.update(zip(ds, outs))
    received = [shares_out[0]] + [moved(shares_out[d], lambda i, r, d=d: (i, r + d)) for d in range(1, reps)]

    panels, results = with_panels(
        functools.partial(middle_kernel, reps), "middle", panels, [*received, weight, upstream, train_mask.reshape(1, share)],
        [
            jax.ShapeDtypeStruct((share, width), bf16),
            jax.ShapeDtypeStruct((width, share), bf16),
            jax.ShapeDtypeStruct((width, width), f32),
        ]
        + [jax.ShapeDtypeStruct((width + width // reps, share), bf16)] * (reps - 1),
        12,
    )
    activated, back, term, *sends = results
    backs = [back] + [moved(send, lambda i, r, d=d: (i, r + d)) for d, send in enumerate(sends, 1)]

    shares = tuple(range(reps))
    head, tail = shares[:4], shares[4:]
    halves = shares[: reps // 2], shares[reps // 2 :]
    sums = jax.ShapeDtypeStruct((reps, width, share), f32)
    panels, (late_sum, early_sum) = with_panels(
        functools.partial(heads_kernel, reps, head), "heads", panels, backs[:4], [sums, sums], 12, flops
    )
    piece_out = pltpu.VMEM((reps // 2, width, share), bf16)
    strip_out = jax.ShapeDtypeStruct((rows_n // 2, width // reps, width), bf16)
    panels, (piece, strips) = with_panels(
        functools.partial(tails_strip_kernel, 1, reps, tail, halves[0]), "late_strip", panels,
        [late_sum, *backs[4:], term, *backs[1:4]], [piece_out, strip_out], 12, flops // 4,
    )
    first = moved(piece, lambda i, r: (i - 1, r) if i % 2 else (i + 1, r + 1))
    panels, (piece,) = with_panels(
        functools.partial(tails_kernel, 1, reps, tail, halves[1]), "late", panels, [late_sum, *backs[4:]], [piece_out], 12, flops // 4
    )
    second = moved(piece, lambda i, r: (i - 1, r))
    panels, (own,) = with_panels(
        functools.partial(tails_kernel, 0, reps, tail, shares), "early", panels, [early_sum, *backs[4:]], [sums], 12, flops // 2
    )
    strips, own = lax.optimization_barrier((strips, own))
    same_core = [[i * reps + r for i in range(c, rows_n, 2)] for c in range(2) for r in range(reps)]
    strips = lax.all_to_all(strips + moved(strips, lambda i, r: (i ^ 1, r)), ("row", "rep"), 0, 0, axis_index_groups=same_core)

    merged = merge(own, first, second, strips)
    got = [moved(merged[d], lambda i, r, d=d: (i - sections * r, r + d)) for d in shares]
    feature_grad, whole = finish(1.0 / math.sqrt(features.shape[0] * rows_n), width, got)
    return activated, whole, feature_grad


def solution(mesh):
    placed = (
        P("row", None),
        P(),
        P("row", "rep", None, None, None, None),
        P("row", "rep", None, None),
        P("row", "rep", None, None),
        P("row", "rep", None),
        P(("row", "rep")),
        P(("row", "rep"), None),
    )
    return jax.shard_map(
        per_device,
        mesh=mesh,
        in_specs=placed,
        out_specs=(P(("row", "rep"), None), P(), P(("row", "rep"), None)),
        check_vma=False,
    )
```

time: 178 us -> 136 us (0.76)
  waiting for transfers between devices: 56.4 us -> 32.7 us
  local copies, waits for them, and re-layouts: 23.9 us -> 2.03 us
  blocking collectives: 0 us -> 11.5 us
  starting transfers between devices: 80.1 us -> 69.4 us
  Pallas kernels: 16.8 us -> 19.1 us
    ppermute x32 -> x25, waiting for transfers between devices: 56.4 us -> 20.2 us  [moved(): return lax.ppermute(value, ('row', 'rep'), pairs(rows_n, reps, target))]
    unnamed x20 -> x12, local copies, waits for them, and re-layouts: 23.9 us -> 2.03 us
    ppermute x32 -> x25, starting transfers between devices: 80.1 us -> 58.4 us  [moved(): return lax.ppermute(value, ('row', 'rep'), pairs(rows_n, reps, target))]
    ppermute x0 -> x3, waiting for transfers between devices: none -> 12.5 us  [the longest x2 12.5 us: fetched(): return lax.ppermute(value, ('row', 'rep'), found)]
    all_to_all x0 -> x1, blocking collectives: none -> 11.5 us  [per_device(): lax.all_to_all(strips + moved(strips, lambda i, r: (i ^ 1, r)), ('row', '...]
    ppermute x0 -> x3, starting transfers between devices: none -> 11 us  [the longest x2 9.7 us: fetched(): return lax.ppermute(value, ('row', 'rep'), found)]
    pallas_call x7 -> x12, Pallas kernels: 16.8 us -> 19.1 us  [the longest x8 10.8 us: with_panels(): pl.pallas_call(kernel, in_specs=[VMEM] * (1 + len(operands)), out_specs=[...]
  transfers between devices with their start and end apart: 32 -> 28, of which waited for: 14 -> 11; matrix products, arithmetic and copies ran while one was open for 1% -> 0% of each run, Pallas kernels for 5% -> 10%
where the time goes in v2:
time: 136 us
  starting transfers between devices  69.4 us (51%)
  waiting for transfers between devices  32.7 us (24%)
  Pallas kernels  19.1 us (14%)
  blocking collectives  11.5 us (8%)
  local copies, waits for them, and re-layouts  2.03 us (1%)
    ppermute x25, starting transfers between devices, moved(): return lax.ppermute(value, ('row', 'rep'), pairs(rows_n, reps, target))  58.4 us
    ppermute x25, waiting for transfers between devices, moved(): return lax.ppermute(value, ('row', 'rep'), pairs(rows_n, reps, target))  20.2 us
    ppermute x2, waiting for transfers between devices, fetched(): return lax.ppermute(value, ('row', 'rep'), found)  12.5 us
    all_to_all x1, blocking collectives, per_device(): lax.all_to_all(strips + moved(strips, lambda i, r: (i ^ 1, r)), ('row', '...  11.5 us
    pallas_call x8, Pallas kernels, with_panels(): pl.pallas_call(kernel, in_specs=[VMEM] * (1 + len(operands)), out_specs=[...  10.8 us
    ppermute x2, starting transfers between devices, fetched(): return lax.ppermute(value, ('row', 'rep'), found)  9.7 us
    pallas_call x2, Pallas kernels, build(): pl.pallas_call(functools.partial(build_kernel, part), grid_spec=pltpu.Pre...  7.21 us
  transfers between devices with their start and end apart: 28, of which 11 were waited for; matrix products, arithmetic and copies ran while one was open for 0% of the time, Pallas kernels for 10%

profile of v2, /device:TPU:8, one launch (start us, length us, event | category | flops | bytes accessed | tf_op | source)
XLA Modules:
  0.0 135.6 jit_solution(3925955581812251199)
XLA Ops:
  0.6 8.4 %collective-permute-start = (bf16[2048,256]{1,0:T(8,128)(2,1)}, bf16[2048,256]{1,0:T(8,128)(2,1)S(1)}, u32[]{:S(2)}, u32[]{:S(2)}) collective-permute-start(bf16[2048,256]{1,0:T(8,128)(2,1)} %param.8), channel_id=1, source_target_pairs={{0,0},{117,1},{98,2},{84,3},{71,4},{49,5},{38,6},{19,7},{8,8},{125... | collective-permute-start | bytes 3145736 | tf_op jit(solution)/shard_map/ppermute | solution.py:268
  11.1 3.5 %build.2 = (bf16[2,16,2048,128]{3,2,1,0:T(8,128)(2,1)S(1)}, s32[8,128]{1,0:T(8,128)S(1)}) custom-call(s32[2,192]{1,0:T(2,128)S(1)} %bitcast.5, s32[2,192]{1,0:T(2,128)S(1)} %bitcast.7, s32[2]{0:T(128)S(1)} %bitcast.9, bf16[2,192,128,128]{3,2,1,0:T(8,128)(2,1)} %bitcast.12), custom_call_target="tpu_custom_call" | custom-call | bytes 15728640 | tf_op jit(solution)/shard_map/build/pallas_call | solution.py:57
  15.9 3.7 %build.3 = (bf16[2,16,2048,128]{3,2,1,0:T(8,128)(2,1)S(1)}, s32[8,128]{1,0:T(8,128)S(1)}) custom-call(s32[2,192]{1,0:T(2,128)S(1)} %bitcast.6, s32[2,192]{1,0:T(2,128)S(1)} %bitcast.8, s32[2]{0:T(128)S(1)} %bitcast.10, bf16[2,192,128,128]{3,2,1,0:T(8,128)(2,1)} %bitcast.13, ...), custom_call_target="tpu_custom_call", output_to_operand_aliasing={{0}: (4, {})} | custom-call | bytes 15728640 | tf_op jit(solution)/shard_map/build/pallas_call | solution.py:57
  19.6 12.5 %collective-permute-done.source = bf16[2048,256]{1,0:T(8,128)(2,1)S(1)} collective-permute-done((bf16[2048,256]{1,0:T(8,128)(2,1)}, bf16[2048,256]{1,0:T(8,128)(2,1)S(1)}, u32[]{:S(2)}, u32[]{:S(2)}) %collective-permute-start) | collective-permute-done | bytes 1048608 | tf_op jit(solution)/shard_map/ppermute | solution.py:268
  33.5 2.3 %first.1 = (bf16[2,16,2048,128]{3,2,1,0:T(8,128)(2,1)S(1)}, f32[8,256,256]{2,1,0:T(8,128)S(1)}) custom-call(bf16[2,16,2048,128]{3,2,1,0:T(8,128)(2,1)S(1)} %get-tuple-element.58.panels, bf16[2048,256]{1,0:T(8,128)(2,1)S(1)} %collective-permute-done.source, s32[8,128]{1,0:T(8,128)S(1)} %get-tuple-element.61.token), custom_call_target="tpu_custom_call", output_to_operand_aliasing={{0}: (0, {})} | custom-call | flops 2147483648 | bytes 2097152 | tf_op jit(solution)/shard_map/first/pallas_call | solution.py:81
  39.3 2.3 %collective-permute-start.8 = (bf16[256,256]{1,0:T(8,128)(2,1)S(1)}, bf16[256,256]{1,0:T(8,128)(2,1)S(1)}, u32[]{:S(2)}, u32[]{:S(2)}) collective-permute-start(bf16[256,256]{1,0:T(8,128)(2,1)S(1)} %get-tuple-element.73), channel_id=1, source_target_pairs={{0,6},{1,7},{2,0},{3,1},{4,2},{5,3},{6,4},{7,5},{8,14},{9,15},{10,... | collective-permute-start | bytes 393224 | tf_op jit(solution)/shard_map/ppermute | solution.py:259
  41.6 3.9 %collective-permute-start.9 = (bf16[256,256]{1,0:T(8,128)(2,1)S(1)}, bf16[256,256]{1,0:T(8,128)(2,1)S(1)}, u32[]{:S(2)}, u32[]{:S(2)}) collective-permute-start(bf16[256,256]{1,0:T(8,128)(2,1)S(1)} %get-tuple-element.74), channel_id=1, source_target_pairs={{0,7},{1,0},{2,1},{3,2},{4,3},{5,4},{6,5},{7,6},{8,15},{9,8},{10,9... | collective-permute-start | bytes 393224 | tf_op jit(solution)/shard_map/ppermute | solution.py:259
  47.6 4.2 %collective-permute-start.6 = (bf16[256,256]{1,0:T(8,128)(2,1)S(1)}, bf16[256,256]{1,0:T(8,128)(2,1)S(1)}, u32[]{:S(2)}, u32[]{:S(2)}) collective-permute-start(bf16[256,256]{1,0:T(8,128)(2,1)S(1)} %get-tuple-element.71), channel_id=1, source_target_pairs={{0,4},{1,5},{2,6},{3,7},{4,0},{5,1},{6,2},{7,3},{8,12},{9,13},{10,... | collective-permute-start | bytes 393224 | tf_op jit(solution)/shard_map/ppermute | solution.py:259
  55.4 2.6 %collective-permute-done.6.refs_4_ = bf16[256,256]{1,0:T(8,128)(2,1)S(1)} collective-permute-done((bf16[256,256]{1,0:T(8,128)(2,1)S(1)}, bf16[256,256]{1,0:T(8,128)(2,1)S(1)}, u32[]{:S(2)}, u32[]{:S(2)}) %collective-permute-start.6) | collective-permute-done | bytes 131104 | tf_op jit(solution)/shard_map/ppermute | solution.py:259
  59.0 6.2 %collective-permute-start.11 = (bf16[288,256]{1,0:T(8,128)(2,1)S(1)}, bf16[288,256]{1,0:T(8,128)(2,1)S(1)}, u32[]{:S(2)}, u32[]{:S(2)}) collective-permute-start(bf16[288,256]{1,0:T(8,128)(2,1)S(1)} %get-tuple-element.79), channel_id=1, source_target_pairs={{0,2},{1,3},{2,4},{3,5},{4,6},{5,7},{6,0},{7,1},{8,10},{9,11},{10,... | collective-permute-start | bytes 442376 | tf_op jit(solution)/shard_map/ppermute | solution.py:259
  65.1 2.5 %collective-permute-start.13 = (bf16[288,256]{1,0:T(8,128)(2,1)S(1)}, bf16[288,256]{1,0:T(8,128)(2,1)S(1)}, u32[]{:S(2)}, u32[]{:S(2)}) collective-permute-start(bf16[288,256]{1,0:T(8,128)(2,1)S(1)} %get-tuple-element.83), channel_id=1, source_target_pairs={{0,4},{1,5},{2,6},{3,7},{4,0},{5,1},{6,2},{7,3},{8,12},{9,13},{10,... | collective-permute-start | bytes 442376 | tf_op jit(solution)/shard_map/ppermute | solution.py:259
  67.6 2.9 %collective-permute-start.14 = (bf16[288,256]{1,0:T(8,128)(2,1)S(1)}, bf16[288,256]{1,0:T(8,128)(2,1)S(1)}, u32[]{:S(2)}, u32[]{:S(2)}) collective-permute-start(bf16[288,256]{1,0:T(8,128)(2,1)S(1)} %get-tuple-element.84), channel_id=1, source_target_pairs={{0,5},{1,6},{2,7},{3,0},{4,1},{5,2},{6,3},{7,4},{8,13},{9,14},{10,... | collective-permute-start | bytes 442376 | tf_op jit(solution)/shard_map/ppermute | solution.py:259
  70.6 4.0 %collective-permute-start.15 = (bf16[288,256]{1,0:T(8,128)(2,1)S(1)}, bf16[288,256]{1,0:T(8,128)(2,1)S(1)}, u32[]{:S(2)}, u32[]{:S(2)}) collective-permute-start(bf16[288,256]{1,0:T(8,128)(2,1)S(1)} %get-tuple-element.85), channel_id=1, source_target_pairs={{0,6},{1,7},{2,0},{3,1},{4,2},{5,3},{6,4},{7,5},{8,14},{9,15},{10,... | collective-permute-start | bytes 442376 | tf_op jit(solution)/shard_map/ppermute | solution.py:259
  74.6 3.0 %collective-permute-start.16 = (bf16[288,256]{1,0:T(8,128)(2,1)S(1)}, bf16[288,256]{1,0:T(8,128)(2,1)S(1)}, u32[]{:S(2)}, u32[]{:S(2)}) collective-permute-start(bf16[288,256]{1,0:T(8,128)(2,1)S(1)} %get-tuple-element.86), channel_id=1, source_target_pairs={{0,7},{1,0},{2,1},{3,2},{4,3},{5,4},{6,5},{7,6},{8,15},{9,8},{10,9... | collective-permute-start | bytes 442376 | tf_op jit(solution)/shard_map/ppermute | solution.py:259
  79.0 2.3 %heads.1 = (bf16[2,16,2048,128]{3,2,1,0:T(8,128)(2,1)S(1)}, f32[8,256,256]{2,1,0:T(8,128)S(1)}, f32[8,256,256]{2,1,0:T(8,128)S(1)}) custom-call(bf16[2,16,2048,128]{3,2,1,0:T(8,128)(2,1)S(1)} %get-tuple-element.76.panels, bf16[256,256]{1,0:T(8,128)(2,1)S(1)} %get-tuple-element.77.refs_0_, ...), custom_call_target="tpu_custom_call", output_to_operand_aliasing={{0}: (0, {})} | custom-call | flops 2147483648 | bytes 2097152 | tf_op jit(solution)/shard_map/heads/pallas_call | solution.py:81
  84.1 3.4 %collective-permute-start.18 = (bf16[4,256,256]{2,1,0:T(8,128)(2,1)S(1)}, bf16[4,256,256]{2,1,0:T(8,128)(2,1)S(1)}, u32[]{:S(2)}, u32[]{:S(2)}) collective-permute-start(bf16[4,256,256]{2,1,0:T(8,128)(2,1)S(1)} %get-tuple-element.95), channel_id=1, source_target_pairs={{0,120},{1,121},{2,122},{3,123},{4,124},{5,125},{6,126},{7,127},{8... | collective-permute-start | bytes 1572872 | tf_op jit(solution)/shard_map/ppermute | solution.py:259
  90.2 11.5 %all_to_all.5.strips = bf16[8,32,256]{2,1,0:T(8,128)(2,1)S(1)} all-to-all(bf16[8,32,256]{2,1,0:T(8,128)(2,1)S(1)} %add.3), channel_id=1, replica_groups={{0,16,32,48,64,80,96,112},{1,17,33,49,65,81,97,113},{2,18,34,50,66,82,9..., dimensions={0} | all-to-all | bytes 262144 | tf_op jit(solution)/shard_map/all_to_all | solution.py:332
  101.9 3.5 %collective-permute-start.20 = (bf16[288,256]{1,0:T(8,128)(2,1)S(1)}, bf16[288,256]{1,0:T(8,128)(2,1)S(1)}, u32[]{:S(2)}, u32[]{:S(2)}) collective-permute-start(bf16[288,256]{1,0:T(8,128)(2,1)S(1)} %get-tuple-element.97), channel_id=1, source_target_pairs={{0,0},{1,113},{2,98},{3,83},{4,68},{5,53},{6,38},{7,23},{8,8},{9,1... | collective-permute-start | bytes 442376 | tf_op jit(solution)/shard_map/ppermute | solution.py:259
  107.2 4.9 %collective-permute-start.22 = (bf16[288,256]{1,0:T(8,128)(2,1)S(1)}, bf16[288,256]{1,0:T(8,128)(2,1)S(1)}, u32[]{:S(2)}, u32[]{:S(2)}) collective-permute-start(bf16[288,256]{1,0:T(8,128)(2,1)S(1)} %get-tuple-element.99), channel_id=1, source_target_pairs={{0,2},{1,115},{2,100},{3,85},{4,70},{5,55},{6,32},{7,17},{8,10},{9... | collective-permute-start | bytes 442376 | tf_op jit(solution)/shard_map/ppermute | solution.py:259
  112.2 3.1 %collective-permute-start.23 = (bf16[288,256]{1,0:T(8,128)(2,1)S(1)}, bf16[288,256]{1,0:T(8,128)(2,1)S(1)}, u32[]{:S(2)}, u32[]{:S(2)}) collective-permute-start(bf16[288,256]{1,0:T(8,128)(2,1)S(1)} %get-tuple-element.100), channel_id=1, source_target_pairs={{0,3},{1,116},{2,101},{3,86},{4,71},{5,48},{6,33},{7,18},{8,11},{9... | collective-permute-start | bytes 442376 | tf_op jit(solution)/shard_map/ppermute | solution.py:259
  117.9 6.4 %collective-permute-start.26 = (bf16[288,256]{1,0:T(8,128)(2,1)S(1)}, bf16[288,256]{1,0:T(8,128)(2,1)S(1)}, u32[]{:S(2)}, u32[]{:S(2)}) collective-permute-start(bf16[288,256]{1,0:T(8,128)(2,1)S(1)} %get-tuple-element.103), channel_id=1, source_target_pairs={{0,6},{1,119},{2,96},{3,81},{4,66},{5,51},{6,36},{7,21},{8,14},{9,... | collective-permute-start | bytes 442376 | tf_op jit(solution)/shard_map/ppermute | solution.py:259
  124.4 2.2 %collective-permute-done.24.refs_4_ = bf16[288,256]{1,0:T(8,128)(2,1)S(1)} collective-permute-done((bf16[288,256]{1,0:T(8,128)(2,1)S(1)}, bf16[288,256]{1,0:T(8,128)(2,1)S(1)}, u32[]{:S(2)}, u32[]{:S(2)}) %collective-permute-start.24) | collective-permute-done | bytes 147488 | tf_op jit(solution)/shard_map/ppermute | solution.py:259
  126.6 2.3 %collective-permute-done.25.refs_5_ = bf16[288,256]{1,0:T(8,128)(2,1)S(1)} collective-permute-done((bf16[288,256]{1,0:T(8,128)(2,1)S(1)}, bf16[288,256]{1,0:T(8,128)(2,1)S(1)}, u32[]{:S(2)}, u32[]{:S(2)}) %collective-permute-start.25) | collective-permute-done | bytes 147488 | tf_op jit(solution)/shard_map/ppermute | solution.py:259
  128.9 5.8 %collective-permute-done.26.refs_6_ = bf16[288,256]{1,0:T(8,128)(2,1)S(1)} collective-permute-done((bf16[288,256]{1,0:T(8,128)(2,1)S(1)}, bf16[288,256]{1,0:T(8,128)(2,1)S(1)}, u32[]{:S(2)}, u32[]{:S(2)}) %collective-permute-start.26) | collective-permute-done | bytes 147488 | tf_op jit(solution)/shard_map/ppermute | solution.py:259
  (58 shorter events, 27.2 us)
Async XLA Ops:
  0.6 31.5 %collective-permute-start = (bf16[2048,256]{1,0:T(8,128)(2,1)}, bf16[2048,256]{1,0:T(8,128)(2,1)S(1)}, u32[]{:S(2)}, u32[]{:S(2)}) collective-permute-start(bf16[2048,256]{1,0:T(8,128)(2,1)} %param.8), channel_id=1, source_target_pairs={{0,0},{117,1},{98,2},{84,3},{71,4},{49,5},{38,6},{19,7},{8,8},{125... | collective-permute-start | bytes 3145736 | tf_op jit(solution)/shard_map/ppermute | solution.py:268
  14.6 21.3 %collective-permute-start.2 = (bf16[2048,256]{1,0:T(8,128)(2,1)}, bf16[2048,256]{1,0:T(8,128)(2,1)S(1)}, u32[]{:S(2)}, u32[]{:S(2)}) collective-permute-start(bf16[2048,256]{1,0:T(8,128)(2,1)} %param.8), channel_id=1, source_target_pairs={{121,0},{110,1},{91,2},{72,3},{61,4},{42,5},{28,6},{15,7},{9,16},{... | collective-permute-start | bytes 3145736 | tf_op jit(solution)/shard_map/ppermute | solution.py:268
  38.4 8.5 %collective-permute-start.7 = (bf16[256,256]{1,0:T(8,128)(2,1)S(1)}, bf16[256,256]{1,0:T(8,128)(2,1)S(1)}, u32[]{:S(2)}, u32[]{:S(2)}) collective-permute-start(bf16[256,256]{1,0:T(8,128)(2,1)S(1)} %get-tuple-element.72), channel_id=1, source_target_pairs={{0,5},{1,6},{2,7},{3,0},{4,1},{5,2},{6,3},{7,4},{8,13},{9,14},{10,... | collective-permute-start | bytes 393224 | tf_op jit(solution)/shard_map/ppermute | solution.py:259
  39.3 8.3 %collective-permute-start.8 = (bf16[256,256]{1,0:T(8,128)(2,1)S(1)}, bf16[256,256]{1,0:T(8,128)(2,1)S(1)}, u32[]{:S(2)}, u32[]{:S(2)}) collective-permute-start(bf16[256,256]{1,0:T(8,128)(2,1)S(1)} %get-tuple-element.73), channel_id=1, source_target_pairs={{0,6},{1,7},{2,0},{3,1},{4,2},{5,3},{6,4},{7,5},{8,14},{9,15},{10,... | collective-permute-start | bytes 393224 | tf_op jit(solution)/shard_map/ppermute | solution.py:259
  41.6 10.2 %collective-permute-start.9 = (bf16[256,256]{1,0:T(8,128)(2,1)S(1)}, bf16[256,256]{1,0:T(8,128)(2,1)S(1)}, u32[]{:S(2)}, u32[]{:S(2)}) collective-permute-start(bf16[256,256]{1,0:T(8,128)(2,1)S(1)} %get-tuple-element.74), channel_id=1, source_target_pairs={{0,7},{1,0},{2,1},{3,2},{4,3},{5,4},{6,5},{7,6},{8,15},{9,8},{10,9... | collective-permute-start | bytes 393224 | tf_op jit(solution)/shard_map/ppermute | solution.py:259
  45.5 8.7 %collective-permute-start.4 = (bf16[256,256]{1,0:T(8,128)(2,1)S(1)}, bf16[256,256]{1,0:T(8,128)(2,1)S(1)}, u32[]{:S(2)}, u32[]{:S(2)}) collective-permute-start(bf16[256,256]{1,0:T(8,128)(2,1)S(1)} %get-tuple-element.69), channel_id=1, source_target_pairs={{0,2},{1,3},{2,4},{3,5},{4,6},{5,7},{6,0},{7,1},{8,10},{9,11},{10,... | collective-permute-start | bytes 393224 | tf_op jit(solution)/shard_map/ppermute | solution.py:259
  46.9 8.5 %collective-permute-start.5 = (bf16[256,256]{1,0:T(8,128)(2,1)S(1)}, bf16[256,256]{1,0:T(8,128)(2,1)S(1)}, u32[]{:S(2)}, u32[]{:S(2)}) collective-permute-start(bf16[256,256]{1,0:T(8,128)(2,1)S(1)} %get-tuple-element.70), channel_id=1, source_target_pairs={{0,3},{1,4},{2,5},{3,6},{4,7},{5,0},{6,1},{7,2},{8,11},{9,12},{10,... | collective-permute-start | bytes 393224 | tf_op jit(solution)/shard_map/ppermute | solution.py:259
  47.6 10.4 %collective-permute-start.6 = (bf16[256,256]{1,0:T(8,128)(2,1)S(1)}, bf16[256,256]{1,0:T(8,128)(2,1)S(1)}, u32[]{:S(2)}, u32[]{:S(2)}) collective-permute-start(bf16[256,256]{1,0:T(8,128)(2,1)S(1)} %get-tuple-element.71), channel_id=1, source_target_pairs={{0,4},{1,5},{2,6},{3,7},{4,0},{5,1},{6,2},{7,3},{8,12},{9,13},{10,... | collective-permute-start | bytes 393224 | tf_op jit(solution)/shard_map/ppermute | solution.py:259
  59.0 11.6 %collective-permute-start.10 = (bf16[288,256]{1,0:T(8,128)(2,1)S(1)}, bf16[288,256]{1,0:T(8,128)(2,1)S(1)}, u32[]{:S(2)}, u32[]{:S(2)}) collective-permute-start(bf16[288,256]{1,0:T(8,128)(2,1)S(1)} %get-tuple-element.78), channel_id=1, source_target_pairs={{0,1},{1,2},{2,3},{3,4},{4,5},{5,6},{6,7},{7,0},{8,9},{9,10},{10,1... | collective-permute-start | bytes 442376 | tf_op jit(solution)/shard_map/ppermute | solution.py:259
  59.0 15.6 %collective-permute-start.11 = (bf16[288,256]{1,0:T(8,128)(2,1)S(1)}, bf16[288,256]{1,0:T(8,128)(2,1)S(1)}, u32[]{:S(2)}, u32[]{:S(2)}) collective-permute-start(bf16[288,256]{1,0:T(8,128)(2,1)S(1)} %get-tuple-element.79), channel_id=1, source_target_pairs={{0,2},{1,3},{2,4},{3,5},{4,6},{5,7},{6,0},{7,1},{8,10},{9,11},{10,... | collective-permute-start | bytes 442376 | tf_op jit(solution)/shard_map/ppermute | solution.py:259
  65.1 13.8 %collective-permute-start.12 = (bf16[288,256]{1,0:T(8,128)(2,1)S(1)}, bf16[288,256]{1,0:T(8,128)(2,1)S(1)}, u32[]{:S(2)}, u32[]{:S(2)}) collective-permute-start(bf16[288,256]{1,0:T(8,128)(2,1)S(1)} %get-tuple-element.80), channel_id=1, source_target_pairs={{0,3},{1,4},{2,5},{3,6},{4,7},{5,0},{6,1},{7,2},{8,11},{9,12},{10,... | collective-permute-start | bytes 442376 | tf_op jit(solution)/shard_map/ppermute | solution.py:259
  65.1 16.2 %collective-permute-start.13 = (bf16[288,256]{1,0:T(8,128)(2,1)S(1)}, bf16[288,256]{1,0:T(8,128)(2,1)S(1)}, u32[]{:S(2)}, u32[]{:S(2)}) collective-permute-start(bf16[288,256]{1,0:T(8,128)(2,1)S(1)} %get-tuple-element.83), channel_id=1, source_target_pairs={{0,4},{1,5},{2,6},{3,7},{4,0},{5,1},{6,2},{7,3},{8,12},{9,13},{10,... | collective-permute-start | bytes 442376 | tf_op jit(solution)/shard_map/ppermute | solution.py:259
  67.6 13.7 %collective-permute-start.14 = (bf16[288,256]{1,0:T(8,128)(2,1)S(1)}, bf16[288,256]{1,0:T(8,128)(2,1)S(1)}, u32[]{:S(2)}, u32[]{:S(2)}) collective-permute-start(bf16[288,256]{1,0:T(8,128)(2,1)S(1)} %get-tuple-element.84), channel_id=1, source_target_pairs={{0,5},{1,6},{2,7},{3,0},{4,1},{5,2},{6,3},{7,4},{8,13},{9,14},{10,... | collective-permute-start | bytes 442376 | tf_op jit(solution)/shard_map/ppermute | solution.py:259
  70.6 10.8 %collective-permute-start.15 = (bf16[288,256]{1,0:T(8,128)(2,1)S(1)}, bf16[288,256]{1,0:T(8,128)(2,1)S(1)}, u32[]{:S(2)}, u32[]{:S(2)}) collective-permute-start(bf16[288,256]{1,0:T(8,128)(2,1)S(1)} %get-tuple-element.85), channel_id=1, source_target_pairs={{0,6},{1,7},{2,0},{3,1},{4,2},{5,3},{6,4},{7,5},{8,14},{9,15},{10,... | collective-permute-start | bytes 442376 | tf_op jit(solution)/shard_map/ppermute | solution.py:259
  82.9 18.8 %collective-permute-start.17 = (bf16[4,256,256]{2,1,0:T(8,128)(2,1)S(1)}, bf16[4,256,256]{2,1,0:T(8,128)(2,1)S(1)}, u32[]{:S(2)}, u32[]{:S(2)}) collective-permute-start(bf16[4,256,256]{2,1,0:T(8,128)(2,1)S(1)} %get-tuple-element.94), channel_id=1, source_target_pairs={{0,9},{1,10},{2,11},{3,12},{4,13},{5,14},{6,15},{7,8},{8,0},{9,1},... | collective-permute-start | bytes 1572872 | tf_op jit(solution)/shard_map/ppermute | solution.py:259
  84.1 17.6 %collective-permute-start.18 = (bf16[4,256,256]{2,1,0:T(8,128)(2,1)S(1)}, bf16[4,256,256]{2,1,0:T(8,128)(2,1)S(1)}, u32[]{:S(2)}, u32[]{:S(2)}) collective-permute-start(bf16[4,256,256]{2,1,0:T(8,128)(2,1)S(1)} %get-tuple-element.95), channel_id=1, source_target_pairs={{0,120},{1,121},{2,122},{3,123},{4,124},{5,125},{6,126},{7,127},{8... | collective-permute-start | bytes 1572872 | tf_op jit(solution)/shard_map/ppermute | solution.py:259
  101.9 14.1 %collective-permute-start.20 = (bf16[288,256]{1,0:T(8,128)(2,1)S(1)}, bf16[288,256]{1,0:T(8,128)(2,1)S(1)}, u32[]{:S(2)}, u32[]{:S(2)}) collective-permute-start(bf16[288,256]{1,0:T(8,128)(2,1)S(1)} %get-tuple-element.97), channel_id=1, source_target_pairs={{0,0},{1,113},{2,98},{3,83},{4,68},{5,53},{6,38},{7,23},{8,8},{9,1... | collective-permute-start | bytes 442376 | tf_op jit(solution)/shard_map/ppermute | solution.py:259
  105.5 12.5 %collective-permute-start.21 = (bf16[288,256]{1,0:T(8,128)(2,1)S(1)}, bf16[288,256]{1,0:T(8,128)(2,1)S(1)}, u32[]{:S(2)}, u32[]{:S(2)}) collective-permute-start(bf16[288,256]{1,0:T(8,128)(2,1)S(1)} %get-tuple-element.98), channel_id=1, source_target_pairs={{0,1},{1,114},{2,99},{3,84},{4,69},{5,54},{6,39},{7,16},{8,9},{9,1... | collective-permute-start | bytes 442376 | tf_op jit(solution)/shard_map/ppermute | solution.py:259
  107.2 17.1 %collective-permute-start.22 = (bf16[288,256]{1,0:T(8,128)(2,1)S(1)}, bf16[288,256]{1,0:T(8,128)(2,1)S(1)}, u32[]{:S(2)}, u32[]{:S(2)}) collective-permute-start(bf16[288,256]{1,0:T(8,128)(2,1)S(1)} %get-tuple-element.99), channel_id=1, source_target_pairs={{0,2},{1,115},{2,100},{3,85},{4,70},{5,55},{6,32},{7,17},{8,10},{9... | collective-permute-start | bytes 442376 | tf_op jit(solution)/shard_map/ppermute | solution.py:259
  112.2 12.2 %collective-permute-start.23 = (bf16[288,256]{1,0:T(8,128)(2,1)S(1)}, bf16[288,256]{1,0:T(8,128)(2,1)S(1)}, u32[]{:S(2)}, u32[]{:S(2)}) collective-permute-start(bf16[288,256]{1,0:T(8,128)(2,1)S(1)} %get-tuple-element.100), channel_id=1, source_target_pairs={{0,3},{1,116},{2,101},{3,86},{4,71},{5,48},{6,33},{7,18},{8,11},{9... | collective-permute-start | bytes 442376 | tf_op jit(solution)/shard_map/ppermute | solution.py:259
  115.3 11.3 %collective-permute-start.24 = (bf16[288,256]{1,0:T(8,128)(2,1)S(1)}, bf16[288,256]{1,0:T(8,128)(2,1)S(1)}, u32[]{:S(2)}, u32[]{:S(2)}) collective-permute-start(bf16[288,256]{1,0:T(8,128)(2,1)S(1)} %get-tuple-element.101), channel_id=1, source_target_pairs={{0,4},{1,117},{2,102},{3,87},{4,64},{5,49},{6,34},{7,19},{8,12},{9... | collective-permute-start | bytes 442376 | tf_op jit(solution)/shard_map/ppermute | solution.py:259
  116.0 12.9 %collective-permute-start.25 = (bf16[288,256]{1,0:T(8,128)(2,1)S(1)}, bf16[288,256]{1,0:T(8,128)(2,1)S(1)}, u32[]{:S(2)}, u32[]{:S(2)}) collective-permute-start(bf16[288,256]{1,0:T(8,128)(2,1)S(1)} %get-tuple-element.102), channel_id=1, source_target_pairs={{0,5},{1,118},{2,103},{3,80},{4,65},{5,50},{6,35},{7,20},{8,13},{9... | collective-permute-start | bytes 442376 | tf_op jit(solution)/shard_map/ppermute | solution.py:259
  117.9 16.8 %collective-permute-start.26 = (bf16[288,256]{1,0:T(8,128)(2,1)S(1)}, bf16[288,256]{1,0:T(8,128)(2,1)S(1)}, u32[]{:S(2)}, u32[]{:S(2)}) collective-permute-start(bf16[288,256]{1,0:T(8,128)(2,1)S(1)} %get-tuple-element.103), channel_id=1, source_target_pairs={{0,6},{1,119},{2,96},{3,81},{4,66},{5,51},{6,36},{7,21},{8,14},{9,... | collective-permute-start | bytes 442376 | tf_op jit(solution)/shard_map/ppermute | solution.py:259
  124.4 10.3 %collective-permute-start.27 = (bf16[288,256]{1,0:T(8,128)(2,1)S(1)}, bf16[288,256]{1,0:T(8,128)(2,1)S(1)}, u32[]{:S(2)}, u32[]{:S(2)}) collective-permute-start(bf16[288,256]{1,0:T(8,128)(2,1)S(1)} %get-tuple-element.104), channel_id=1, source_target_pairs={{0,7},{1,112},{2,97},{3,82},{4,67},{5,52},{6,37},{7,22},{8,15},{9,... | collective-permute-start | bytes 442376 | tf_op jit(solution)/shard_map/ppermute | solution.py:259
  (10 other events, 88.3 us)

commit v3 on v2

--- a/solution.py
+++ b/solution.py
@@ -113,9 +113,17 @@
         out[...] = total.astype(out.dtype)
 
 
-def middle_kernel(shares, panels, *refs):
-    parts = refs[:shares]
-    weight, upstream, train_mask, same, activated, back, term, *sends = refs[shares:]
+def sum_kernel(panels, *refs):
+    parts, (same, out) = refs[:-2], refs[-2:]
+    total = parts[0][...].astype(jnp.float32)
+    for part in parts[1:]:
+        total += part[...].astype(jnp.float32)
+    out[...] = total
+
+
+def middle_kernel(shares, count, panels, *refs):
+    parts = refs[:count]
+    weight, upstream, train_mask, same, activated, back, term, *sends = refs[count:]
     replica, _ = place_of()
     total = parts[0][...].astype(jnp.float32)
     for part in parts[1:]:
@@ -244,8 +252,8 @@
     return found
 
 
-MAIN_FROM = (0, 5, 2, 4, 7, 1, 6, 3)
-OTHER_FROM = (1, 6, 3, 0, 5, 2, 4, 7)
+MAIN_FROM = (0, 5, 2, 7, 4, 1, 6, 3)
+OTHER_FROM = (1, 6, 3, 0, 5, 2, 7, 4)
 
 
 def per_device(features, weight, tile_values, tile_rows, tile_cols, tile_count, train_mask, upstream):
@@ -292,9 +300,12 @@
         )
         shares_out.update(zip(ds, outs))
     received = [shares_out[0]] + [moved(shares_out[d], lambda i, r, d=d: (i, r + d)) for d in range(1, reps)]
+    half = reps // 2 + 1
+    panels, (some,) = with_panels(sum_kernel, "some", panels, received[1:half], [jax.ShapeDtypeStruct((share, width), f32)], 12)
+    received = [some, shares_out[0], *received[half:]]
 
     panels, results = with_panels(
-        functools.partial(middle_kernel, reps), "middle", panels, [*received, weight, upstream, train_mask.reshape(1, share)],
+        functools.partial(middle_kernel, reps, len(received)), "middle", panels, [*received, weight, upstream, train_mask.reshape(1, share)],
         [
             jax.ShapeDtypeStruct((share, width), bf16),
             jax.ShapeDtypeStruct((width, share), bf16),

time: 136 us -> 130 us (0.956)
  starting transfers between devices: 69.4 us -> 65.7 us
  waiting for transfers between devices: 32.7 us -> 30.8 us
    ppermute x25, starting transfers between devices: 58.4 us -> 54.6 us  [moved(): return lax.ppermute(value, ('row', 'rep'), pairs(rows_n, reps, target))]
    ppermute x25, waiting for transfers between devices: 20.2 us -> 18.7 us  [moved(): return lax.ppermute(value, ('row', 'rep'), pairs(rows_n, reps, target))]
    pallas_call x8 -> x9, Pallas kernels: 10.8 us -> 10.8 us  [with_panels(): pl.pallas_call(kernel, in_specs=[VMEM] * (1 + len(operands)), out_specs=[...]
  transfers between devices with their start and end apart: 28 -> 28, of which waited for: 11 -> 12; matrix products, arithmetic and copies ran while one was open for 0% -> 0% of each run, Pallas kernels for 10% -> 12%
where the time goes in v3:
time: 130 us; the launch traced here: 129 us
  starting transfers between devices  65.7 us (51%)
  waiting for transfers between devices  30.8 us (24%)
  Pallas kernels  19.7 us (15%)
  blocking collectives  10.5 us (8%)
  local copies, waits for them, and re-layouts  2.02 us (2%)
    ppermute x25, starting transfers between devices, moved(): return lax.ppermute(value, ('row', 'rep'), pairs(rows_n, reps, target))  54.6 us
    ppermute x25, waiting for transfers between devices, moved(): return lax.ppermute(value, ('row', 'rep'), pairs(rows_n, reps, target))  18.7 us
    ppermute x2, waiting for transfers between devices, fetched(): return lax.ppermute(value, ('row', 'rep'), found)  12.1 us
    pallas_call x9, Pallas kernels, with_panels(): pl.pallas_call(kernel, in_specs=[VMEM] * (1 + len(operands)), out_specs=[...  10.8 us
    all_to_all x1, blocking collectives, per_device(): lax.all_to_all(strips + moved(strips, lambda i, r: (i ^ 1, r)), ('row', '...  10.5 us
    ppermute x2, starting transfers between devices, fetched(): return lax.ppermute(value, ('row', 'rep'), found)  9.7 us
    pallas_call x2, Pallas kernels, build(): pl.pallas_call(functools.partial(build_kernel, part), grid_spec=pltpu.Pre...  7.69 us
  transfers between devices with their start and end apart: 28, of which 12 were waited for; matrix products, arithmetic and copies ran while one was open for 0% of the time, Pallas kernels for 12%

profile of v3, /device:TPU:8, one launch (start us, length us, event | category | flops | bytes accessed | tf_op | source)
XLA Modules:
  0.0 129.5 jit_solution(4557551834577907945)
XLA Ops:
  0.6 8.4 %collective-permute-start = (bf16[2048,256]{1,0:T(8,128)(2,1)}, bf16[2048,256]{1,0:T(8,128)(2,1)S(1)}, u32[]{:S(2)}, u32[]{:S(2)}) collective-permute-start(bf16[2048,256]{1,0:T(8,128)(2,1)} %param.8), channel_id=1, source_target_pairs={{0,0},{117,1},{98,2},{87,3},{68,4},{49,5},{38,6},{19,7},{8,8},{125... | collective-permute-start | bytes 3145736 | tf_op jit(solution)/shard_map/ppermute | solution.py:276
  11.1 3.5 %build.2 = (bf16[2,16,2048,128]{3,2,1,0:T(8,128)(2,1)S(1)}, s32[8,128]{1,0:T(8,128)S(1)}) custom-call(s32[2,192]{1,0:T(2,128)S(1)} %bitcast.5, s32[2,192]{1,0:T(2,128)S(1)} %bitcast.7, s32[2]{0:T(128)S(1)} %bitcast.9, bf16[2,192,128,128]{3,2,1,0:T(8,128)(2,1)} %bitcast.12), custom_call_target="tpu_custom_call" | custom-call | bytes 15728640 | tf_op jit(solution)/shard_map/build/pallas_call | solution.py:57
  15.9 4.2 %build.3 = (bf16[2,16,2048,128]{3,2,1,0:T(8,128)(2,1)S(1)}, s32[8,128]{1,0:T(8,128)S(1)}) custom-call(s32[2,192]{1,0:T(2,128)S(1)} %bitcast.6, s32[2,192]{1,0:T(2,128)S(1)} %bitcast.8, s32[2]{0:T(128)S(1)} %bitcast.10, bf16[2,192,128,128]{3,2,1,0:T(8,128)(2,1)} %bitcast.13, ...), custom_call_target="tpu_custom_call", output_to_operand_aliasing={{0}: (4, {})} | custom-call | bytes 15728640 | tf_op jit(solution)/shard_map/build/pallas_call | solution.py:57
  20.1 12.1 %collective-permute-done.source = bf16[2048,256]{1,0:T(8,128)(2,1)S(1)} collective-permute-done((bf16[2048,256]{1,0:T(8,128)(2,1)}, bf16[2048,256]{1,0:T(8,128)(2,1)S(1)}, u32[]{:S(2)}, u32[]{:S(2)}) %collective-permute-start) | collective-permute-done | bytes 1048608 | tf_op jit(solution)/shard_map/ppermute | solution.py:276
  33.5 2.3 %first.1 = (bf16[2,16,2048,128]{3,2,1,0:T(8,128)(2,1)S(1)}, f32[8,256,256]{2,1,0:T(8,128)S(1)}) custom-call(bf16[2,16,2048,128]{3,2,1,0:T(8,128)(2,1)S(1)} %get-tuple-element.60.panels, bf16[2048,256]{1,0:T(8,128)(2,1)S(1)} %collective-permute-done.source, s32[8,128]{1,0:T(8,128)S(1)} %get-tuple-element.63.token), custom_call_target="tpu_custom_call", output_to_operand_aliasing={{0}: (0, {})} | custom-call | flops 2147483648 | bytes 2097152 | tf_op jit(solution)/shard_map/first/pallas_call | solution.py:81
  37.2 3.4 %collective-permute-start.4 = (bf16[256,256]{1,0:T(8,128)(2,1)S(1)}, bf16[256,256]{1,0:T(8,128)(2,1)S(1)}, u32[]{:S(2)}, u32[]{:S(2)}) collective-permute-start(bf16[256,256]{1,0:T(8,128)(2,1)S(1)} %get-tuple-element.70), channel_id=1, source_target_pairs={{0,2},{1,3},{2,4},{3,5},{4,6},{5,7},{6,0},{7,1},{8,10},{9,11},{10,... | collective-permute-start | bytes 393224 | tf_op jit(solution)/shard_map/ppermute | solution.py:267
  42.9 2.0 %collective-permute-start.5 = (bf16[256,256]{1,0:T(8,128)(2,1)S(1)}, bf16[256,256]{1,0:T(8,128)(2,1)S(1)}, u32[]{:S(2)}, u32[]{:S(2)}) collective-permute-start(bf16[256,256]{1,0:T(8,128)(2,1)S(1)} %get-tuple-element.71), channel_id=1, source_target_pairs={{0,3},{1,4},{2,5},{3,6},{4,7},{5,0},{6,1},{7,2},{8,11},{9,12},{10,... | collective-permute-start | bytes 393224 | tf_op jit(solution)/shard_map/ppermute | solution.py:267
  46.0 2.0 %collective-permute-start.8 = (bf16[256,256]{1,0:T(8,128)(2,1)S(1)}, bf16[256,256]{1,0:T(8,128)(2,1)S(1)}, u32[]{:S(2)}, u32[]{:S(2)}) collective-permute-start(bf16[256,256]{1,0:T(8,128)(2,1)S(1)} %get-tuple-element.77), channel_id=1, source_target_pairs={{0,6},{1,7},{2,0},{3,1},{4,2},{5,3},{6,4},{7,5},{8,14},{9,15},{10,... | collective-permute-start | bytes 393224 | tf_op jit(solution)/shard_map/ppermute | solution.py:267
  48.9 4.0 %collective-permute-done.5.refs_2_ = bf16[256,256]{1,0:T(8,128)(2,1)S(1)} collective-permute-done((bf16[256,256]{1,0:T(8,128)(2,1)S(1)}, bf16[256,256]{1,0:T(8,128)(2,1)S(1)}, u32[]{:S(2)}, u32[]{:S(2)}) %collective-permute-start.5) | collective-permute-done | bytes 131104 | tf_op jit(solution)/shard_map/ppermute | solution.py:267
  55.2 2.2 %collective-permute-start.10 = (bf16[288,256]{1,0:T(8,128)(2,1)S(1)}, bf16[288,256]{1,0:T(8,128)(2,1)S(1)}, u32[]{:S(2)}, u32[]{:S(2)}) collective-permute-start(bf16[288,256]{1,0:T(8,128)(2,1)S(1)} %get-tuple-element.82), channel_id=1, source_target_pairs={{0,1},{1,2},{2,3},{3,4},{4,5},{5,6},{6,7},{7,0},{8,9},{9,10},{10,1... | collective-permute-start | bytes 442376 | tf_op jit(solution)/shard_map/ppermute | solution.py:267
  57.4 2.2 %collective-permute-start.11 = (bf16[288,256]{1,0:T(8,128)(2,1)S(1)}, bf16[288,256]{1,0:T(8,128)(2,1)S(1)}, u32[]{:S(2)}, u32[]{:S(2)}) collective-permute-start(bf16[288,256]{1,0:T(8,128)(2,1)S(1)} %get-tuple-element.83), channel_id=1, source_target_pairs={{0,2},{1,3},{2,4},{3,5},{4,6},{5,7},{6,0},{7,1},{8,10},{9,11},{10,... | collective-permute-start | bytes 442376 | tf_op jit(solution)/shard_map/ppermute | solution.py:267
  59.6 3.0 %collective-permute-start.12 = (bf16[288,256]{1,0:T(8,128)(2,1)S(1)}, bf16[288,256]{1,0:T(8,128)(2,1)S(1)}, u32[]{:S(2)}, u32[]{:S(2)}) collective-permute-start(bf16[288,256]{1,0:T(8,128)(2,1)S(1)} %get-tuple-element.84), channel_id=1, source_target_pairs={{0,3},{1,4},{2,5},{3,6},{4,7},{5,0},{6,1},{7,2},{8,11},{9,12},{10,... | collective-permute-start | bytes 442376 | tf_op jit(solution)/shard_map/ppermute | solution.py:267
  63.7 3.6 %collective-permute-start.15 = (bf16[288,256]{1,0:T(8,128)(2,1)S(1)}, bf16[288,256]{1,0:T(8,128)(2,1)S(1)}, u32[]{:S(2)}, u32[]{:S(2)}) collective-permute-start(bf16[288,256]{1,0:T(8,128)(2,1)S(1)} %get-tuple-element.89), channel_id=1, source_target_pairs={{0,6},{1,7},{2,0},{3,1},{4,2},{5,3},{6,4},{7,5},{8,14},{9,15},{10,... | collective-permute-start | bytes 442376 | tf_op jit(solution)/shard_map/ppermute | solution.py:267
  67.6 3.4 %collective-permute-start.16 = (bf16[288,256]{1,0:T(8,128)(2,1)S(1)}, bf16[288,256]{1,0:T(8,128)(2,1)S(1)}, u32[]{:S(2)}, u32[]{:S(2)}) collective-permute-start(bf16[288,256]{1,0:T(8,128)(2,1)S(1)} %get-tuple-element.90), channel_id=1, source_target_pairs={{0,7},{1,0},{2,1},{3,2},{4,3},{5,4},{6,5},{7,6},{8,15},{9,8},{10,9... | collective-permute-start | bytes 442376 | tf_op jit(solution)/shard_map/ppermute | solution.py:267
  71.0 2.3 %heads.1 = (bf16[2,16,2048,128]{3,2,1,0:T(8,128)(2,1)S(1)}, f32[8,256,256]{2,1,0:T(8,128)S(1)}, f32[8,256,256]{2,1,0:T(8,128)S(1)}) custom-call(bf16[2,16,2048,128]{3,2,1,0:T(8,128)(2,1)S(1)} %get-tuple-element.80.panels, bf16[256,256]{1,0:T(8,128)(2,1)S(1)} %get-tuple-element.81.refs_0_, ...), custom_call_target="tpu_custom_call", output_to_operand_aliasing={{0}: (0, {})} | custom-call | flops 2147483648 | bytes 2097152 | tf_op jit(solution)/shard_map/heads/pallas_call | solution.py:81
  76.7 5.9 %collective-permute-start.18 = (bf16[4,256,256]{2,1,0:T(8,128)(2,1)S(1)}, bf16[4,256,256]{2,1,0:T(8,128)(2,1)S(1)}, u32[]{:S(2)}, u32[]{:S(2)}) collective-permute-start(bf16[4,256,256]{2,1,0:T(8,128)(2,1)S(1)} %get-tuple-element.99), channel_id=1, source_target_pairs={{0,120},{1,121},{2,122},{3,123},{4,124},{5,125},{6,126},{7,127},{8... | collective-permute-start | bytes 1572872 | tf_op jit(solution)/shard_map/ppermute | solution.py:267
  85.2 10.5 %all_to_all.5.strips = bf16[8,32,256]{2,1,0:T(8,128)(2,1)S(1)} all-to-all(bf16[8,32,256]{2,1,0:T(8,128)(2,1)S(1)} %add.3), channel_id=1, replica_groups={{0,16,32,48,64,80,96,112},{1,17,33,49,65,81,97,113},{2,18,34,50,66,82,9..., dimensions={0} | all-to-all | bytes 262144 | tf_op jit(solution)/shard_map/all_to_all | solution.py:343
  96.0 3.4 %collective-permute-start.20 = (bf16[288,256]{1,0:T(8,128)(2,1)S(1)}, bf16[288,256]{1,0:T(8,128)(2,1)S(1)}, u32[]{:S(2)}, u32[]{:S(2)}) collective-permute-start(bf16[288,256]{1,0:T(8,128)(2,1)S(1)} %get-tuple-element.101), channel_id=1, source_target_pairs={{0,0},{1,113},{2,98},{3,83},{4,68},{5,53},{6,38},{7,23},{8,8},{9,1... | collective-permute-start | bytes 442376 | tf_op jit(solution)/shard_map/ppermute | solution.py:267
  100.4 5.2 %collective-permute-start.22 = (bf16[288,256]{1,0:T(8,128)(2,1)S(1)}, bf16[288,256]{1,0:T(8,128)(2,1)S(1)}, u32[]{:S(2)}, u32[]{:S(2)}) collective-permute-start(bf16[288,256]{1,0:T(8,128)(2,1)S(1)} %get-tuple-element.103), channel_id=1, source_target_pairs={{0,2},{1,115},{2,100},{3,85},{4,70},{5,55},{6,32},{7,17},{8,10},{9... | collective-permute-start | bytes 442376 | tf_op jit(solution)/shard_map/ppermute | solution.py:267
  105.7 3.2 %collective-permute-start.23 = (bf16[288,256]{1,0:T(8,128)(2,1)S(1)}, bf16[288,256]{1,0:T(8,128)(2,1)S(1)}, u32[]{:S(2)}, u32[]{:S(2)}) collective-permute-start(bf16[288,256]{1,0:T(8,128)(2,1)S(1)} %get-tuple-element.104), channel_id=1, source_target_pairs={{0,3},{1,116},{2,101},{3,86},{4,71},{5,48},{6,33},{7,18},{8,11},{9... | collective-permute-start | bytes 442376 | tf_op jit(solution)/shard_map/ppermute | solution.py:267
  111.6 6.8 %collective-permute-start.26 = (bf16[288,256]{1,0:T(8,128)(2,1)S(1)}, bf16[288,256]{1,0:T(8,128)(2,1)S(1)}, u32[]{:S(2)}, u32[]{:S(2)}) collective-permute-start(bf16[288,256]{1,0:T(8,128)(2,1)S(1)} %get-tuple-element.107), channel_id=1, source_target_pairs={{0,6},{1,119},{2,96},{3,81},{4,66},{5,51},{6,36},{7,21},{8,14},{9,... | collective-permute-start | bytes 442376 | tf_op jit(solution)/shard_map/ppermute | solution.py:267
  118.3 2.2 %collective-permute-done.24.refs_4_ = bf16[288,256]{1,0:T(8,128)(2,1)S(1)} collective-permute-done((bf16[288,256]{1,0:T(8,128)(2,1)S(1)}, bf16[288,256]{1,0:T(8,128)(2,1)S(1)}, u32[]{:S(2)}, u32[]{:S(2)}) %collective-permute-start.24) | collective-permute-done | bytes 147488 | tf_op jit(solution)/shard_map/ppermute | solution.py:267
  120.6 1.5 %collective-permute-done.25.refs_5_ = bf16[288,256]{1,0:T(8,128)(2,1)S(1)} collective-permute-done((bf16[288,256]{1,0:T(8,128)(2,1)S(1)}, bf16[288,256]{1,0:T(8,128)(2,1)S(1)}, u32[]{:S(2)}, u32[]{:S(2)}) %collective-permute-start.25) | collective-permute-done | bytes 147488 | tf_op jit(solution)/shard_map/ppermute | solution.py:267
  122.1 6.5 %collective-permute-done.26.refs_6_ = bf16[288,256]{1,0:T(8,128)(2,1)S(1)} collective-permute-done((bf16[288,256]{1,0:T(8,128)(2,1)S(1)}, bf16[288,256]{1,0:T(8,128)(2,1)S(1)}, u32[]{:S(2)}, u32[]{:S(2)}) %collective-permute-start.26) | collective-permute-done | bytes 147488 | tf_op jit(solution)/shard_map/ppermute | solution.py:267
  (59 shorter events, 24.8 us)
Async XLA Ops:
  0.6 31.5 %collective-permute-start = (bf16[2048,256]{1,0:T(8,128)(2,1)}, bf16[2048,256]{1,0:T(8,128)(2,1)S(1)}, u32[]{:S(2)}, u32[]{:S(2)}) collective-permute-start(bf16[2048,256]{1,0:T(8,128)(2,1)} %param.8), channel_id=1, source_target_pairs={{0,0},{117,1},{98,2},{87,3},{68,4},{49,5},{38,6},{19,7},{8,8},{125... | collective-permute-start | bytes 3145736 | tf_op jit(solution)/shard_map/ppermute | solution.py:276
  14.6 21.3 %collective-permute-start.2 = (bf16[2048,256]{1,0:T(8,128)(2,1)}, bf16[2048,256]{1,0:T(8,128)(2,1)S(1)}, u32[]{:S(2)}, u32[]{:S(2)}) collective-permute-start(bf16[2048,256]{1,0:T(8,128)(2,1)} %param.8), channel_id=1, source_target_pairs={{121,0},{110,1},{91,2},{72,3},{61,4},{42,5},{31,6},{12,7},{9,16},{... | collective-permute-start | bytes 3145736 | tf_op jit(solution)/shard_map/ppermute | solution.py:276
  37.1 8.9 %collective-permute-start.3 = (bf16[256,256]{1,0:T(8,128)(2,1)S(1)}, bf16[256,256]{1,0:T(8,128)(2,1)S(1)}, u32[]{:S(2)}, u32[]{:S(2)}) collective-permute-start(bf16[256,256]{1,0:T(8,128)(2,1)S(1)} %get-tuple-element.69), channel_id=1, source_target_pairs={{0,1},{1,2},{2,3},{3,4},{4,5},{5,6},{6,7},{7,0},{8,9},{9,10},{10,1... | collective-permute-start | bytes 393224 | tf_op jit(solution)/shard_map/ppermute | solution.py:267
  37.2 10.8 %collective-permute-start.4 = (bf16[256,256]{1,0:T(8,128)(2,1)S(1)}, bf16[256,256]{1,0:T(8,128)(2,1)S(1)}, u32[]{:S(2)}, u32[]{:S(2)}) collective-permute-start(bf16[256,256]{1,0:T(8,128)(2,1)S(1)} %get-tuple-element.70), channel_id=1, source_target_pairs={{0,2},{1,3},{2,4},{3,5},{4,6},{5,7},{6,0},{7,1},{8,10},{9,11},{10,... | collective-permute-start | bytes 393224 | tf_op jit(solution)/shard_map/ppermute | solution.py:267
  41.9 11.9 %collective-permute-start.7 = (bf16[256,256]{1,0:T(8,128)(2,1)S(1)}, bf16[256,256]{1,0:T(8,128)(2,1)S(1)}, u32[]{:S(2)}, u32[]{:S(2)}) collective-permute-start(bf16[256,256]{1,0:T(8,128)(2,1)S(1)} %get-tuple-element.76), channel_id=1, source_target_pairs={{0,5},{1,6},{2,7},{3,0},{4,1},{5,2},{6,3},{7,4},{8,13},{9,14},{10,... | collective-permute-start | bytes 393224 | tf_op jit(solution)/shard_map/ppermute | solution.py:267
  42.9 10.0 %collective-permute-start.5 = (bf16[256,256]{1,0:T(8,128)(2,1)S(1)}, bf16[256,256]{1,0:T(8,128)(2,1)S(1)}, u32[]{:S(2)}, u32[]{:S(2)}) collective-permute-start(bf16[256,256]{1,0:T(8,128)(2,1)S(1)} %get-tuple-element.71), channel_id=1, source_target_pairs={{0,3},{1,4},{2,5},{3,6},{4,7},{5,0},{6,1},{7,2},{8,11},{9,12},{10,... | collective-permute-start | bytes 393224 | tf_op jit(solution)/shard_map/ppermute | solution.py:267
  44.9 8.8 %collective-permute-start.6 = (bf16[256,256]{1,0:T(8,128)(2,1)S(1)}, bf16[256,256]{1,0:T(8,128)(2,1)S(1)}, u32[]{:S(2)}, u32[]{:S(2)}) collective-permute-start(bf16[256,256]{1,0:T(8,128)(2,1)S(1)} %get-tuple-element.72), channel_id=1, source_target_pairs={{0,4},{1,5},{2,6},{3,7},{4,0},{5,1},{6,2},{7,3},{8,12},{9,13},{10,... | collective-permute-start | bytes 393224 | tf_op jit(solution)/shard_map/ppermute | solution.py:267
  46.0 7.7 %collective-permute-start.8 = (bf16[256,256]{1,0:T(8,128)(2,1)S(1)}, bf16[256,256]{1,0:T(8,128)(2,1)S(1)}, u32[]{:S(2)}, u32[]{:S(2)}) collective-permute-start(bf16[256,256]{1,0:T(8,128)(2,1)S(1)} %get-tuple-element.77), channel_id=1, source_target_pairs={{0,6},{1,7},{2,0},{3,1},{4,2},{5,3},{6,4},{7,5},{8,14},{9,15},{10,... | collective-permute-start | bytes 393224 | tf_op jit(solution)/shard_map/ppermute | solution.py:267
  55.2 8.5 %collective-permute-start.10 = (bf16[288,256]{1,0:T(8,128)(2,1)S(1)}, bf16[288,256]{1,0:T(8,128)(2,1)S(1)}, u32[]{:S(2)}, u32[]{:S(2)}) collective-permute-start(bf16[288,256]{1,0:T(8,128)(2,1)S(1)} %get-tuple-element.82), channel_id=1, source_target_pairs={{0,1},{1,2},{2,3},{3,4},{4,5},{5,6},{6,7},{7,0},{8,9},{9,10},{10,1... | collective-permute-start | bytes 442376 | tf_op jit(solution)/shard_map/ppermute | solution.py:267
  57.4 10.2 %collective-permute-start.11 = (bf16[288,256]{1,0:T(8,128)(2,1)S(1)}, bf16[288,256]{1,0:T(8,128)(2,1)S(1)}, u32[]{:S(2)}, u32[]{:S(2)}) collective-permute-start(bf16[288,256]{1,0:T(8,128)(2,1)S(1)} %get-tuple-element.83), channel_id=1, source_target_pairs={{0,2},{1,3},{2,4},{3,5},{4,6},{5,7},{6,0},{7,1},{8,10},{9,11},{10,... | collective-permute-start | bytes 442376 | tf_op jit(solution)/shard_map/ppermute | solution.py:267
  59.6 11.4 %collective-permute-start.12 = (bf16[288,256]{1,0:T(8,128)(2,1)S(1)}, bf16[288,256]{1,0:T(8,128)(2,1)S(1)}, u32[]{:S(2)}, u32[]{:S(2)}) collective-permute-start(bf16[288,256]{1,0:T(8,128)(2,1)S(1)} %get-tuple-element.84), channel_id=1, source_target_pairs={{0,3},{1,4},{2,5},{3,6},{4,7},{5,0},{6,1},{7,2},{8,11},{9,12},{10,... | collective-permute-start | bytes 442376 | tf_op jit(solution)/shard_map/ppermute | solution.py:267
  62.6 10.8 %collective-permute-start.13 = (bf16[288,256]{1,0:T(8,128)(2,1)S(1)}, bf16[288,256]{1,0:T(8,128)(2,1)S(1)}, u32[]{:S(2)}, u32[]{:S(2)}) collective-permute-start(bf16[288,256]{1,0:T(8,128)(2,1)S(1)} %get-tuple-element.87), channel_id=1, source_target_pairs={{0,4},{1,5},{2,6},{3,7},{4,0},{5,1},{6,2},{7,3},{8,12},{9,13},{10,... | collective-permute-start | bytes 442376 | tf_op jit(solution)/shard_map/ppermute | solution.py:267
  62.7 10.7 %collective-permute-start.14 = (bf16[288,256]{1,0:T(8,128)(2,1)S(1)}, bf16[288,256]{1,0:T(8,128)(2,1)S(1)}, u32[]{:S(2)}, u32[]{:S(2)}) collective-permute-start(bf16[288,256]{1,0:T(8,128)(2,1)S(1)} %get-tuple-element.88), channel_id=1, source_target_pairs={{0,5},{1,6},{2,7},{3,0},{4,1},{5,2},{6,3},{7,4},{8,13},{9,14},{10,... | collective-permute-start | bytes 442376 | tf_op jit(solution)/shard_map/ppermute | solution.py:267
  63.7 10.3 %collective-permute-start.15 = (bf16[288,256]{1,0:T(8,128)(2,1)S(1)}, bf16[288,256]{1,0:T(8,128)(2,1)S(1)}, u32[]{:S(2)}, u32[]{:S(2)}) collective-permute-start(bf16[288,256]{1,0:T(8,128)(2,1)S(1)} %get-tuple-element.89), channel_id=1, source_target_pairs={{0,6},{1,7},{2,0},{3,1},{4,2},{5,3},{6,4},{7,5},{8,14},{9,15},{10,... | collective-permute-start | bytes 442376 | tf_op jit(solution)/shard_map/ppermute | solution.py:267
  75.5 20.3 %collective-permute-start.17 = (bf16[4,256,256]{2,1,0:T(8,128)(2,1)S(1)}, bf16[4,256,256]{2,1,0:T(8,128)(2,1)S(1)}, u32[]{:S(2)}, u32[]{:S(2)}) collective-permute-start(bf16[4,256,256]{2,1,0:T(8,128)(2,1)S(1)} %get-tuple-element.98), channel_id=1, source_target_pairs={{0,9},{1,10},{2,11},{3,12},{4,13},{5,14},{6,15},{7,8},{8,0},{9,1},... | collective-permute-start | bytes 1572872 | tf_op jit(solution)/shard_map/ppermute | solution.py:267
  76.7 19.1 %collective-permute-start.18 = (bf16[4,256,256]{2,1,0:T(8,128)(2,1)S(1)}, bf16[4,256,256]{2,1,0:T(8,128)(2,1)S(1)}, u32[]{:S(2)}, u32[]{:S(2)}) collective-permute-start(bf16[4,256,256]{2,1,0:T(8,128)(2,1)S(1)} %get-tuple-element.99), channel_id=1, source_target_pairs={{0,120},{1,121},{2,122},{3,123},{4,124},{5,125},{6,126},{7,127},{8... | collective-permute-start | bytes 1572872 | tf_op jit(solution)/shard_map/ppermute | solution.py:267
  96.0 14.3 %collective-permute-start.20 = (bf16[288,256]{1,0:T(8,128)(2,1)S(1)}, bf16[288,256]{1,0:T(8,128)(2,1)S(1)}, u32[]{:S(2)}, u32[]{:S(2)}) collective-permute-start(bf16[288,256]{1,0:T(8,128)(2,1)S(1)} %get-tuple-element.101), channel_id=1, source_target_pairs={{0,0},{1,113},{2,98},{3,83},{4,68},{5,53},{6,38},{7,23},{8,8},{9,1... | collective-permute-start | bytes 442376 | tf_op jit(solution)/shard_map/ppermute | solution.py:267
  99.3 12.3 %collective-permute-start.21 = (bf16[288,256]{1,0:T(8,128)(2,1)S(1)}, bf16[288,256]{1,0:T(8,128)(2,1)S(1)}, u32[]{:S(2)}, u32[]{:S(2)}) collective-permute-start(bf16[288,256]{1,0:T(8,128)(2,1)S(1)} %get-tuple-element.102), channel_id=1, source_target_pairs={{0,1},{1,114},{2,99},{3,84},{4,69},{5,54},{6,39},{7,16},{8,9},{9,1... | collective-permute-start | bytes 442376 | tf_op jit(solution)/shard_map/ppermute | solution.py:267
  100.4 17.9 %collective-permute-start.22 = (bf16[288,256]{1,0:T(8,128)(2,1)S(1)}, bf16[288,256]{1,0:T(8,128)(2,1)S(1)}, u32[]{:S(2)}, u32[]{:S(2)}) collective-permute-start(bf16[288,256]{1,0:T(8,128)(2,1)S(1)} %get-tuple-element.103), channel_id=1, source_target_pairs={{0,2},{1,115},{2,100},{3,85},{4,70},{5,55},{6,32},{7,17},{8,10},{9... | collective-permute-start | bytes 442376 | tf_op jit(solution)/shard_map/ppermute | solution.py:267
  105.7 12.7 %collective-permute-start.23 = (bf16[288,256]{1,0:T(8,128)(2,1)S(1)}, bf16[288,256]{1,0:T(8,128)(2,1)S(1)}, u32[]{:S(2)}, u32[]{:S(2)}) collective-permute-start(bf16[288,256]{1,0:T(8,128)(2,1)S(1)} %get-tuple-element.104), channel_id=1, source_target_pairs={{0,3},{1,116},{2,101},{3,86},{4,71},{5,48},{6,33},{7,18},{8,11},{9... | collective-permute-start | bytes 442376 | tf_op jit(solution)/shard_map/ppermute | solution.py:267
  108.9 11.7 %collective-permute-start.24 = (bf16[288,256]{1,0:T(8,128)(2,1)S(1)}, bf16[288,256]{1,0:T(8,128)(2,1)S(1)}, u32[]{:S(2)}, u32[]{:S(2)}) collective-permute-start(bf16[288,256]{1,0:T(8,128)(2,1)S(1)} %get-tuple-element.105), channel_id=1, source_target_pairs={{0,4},{1,117},{2,102},{3,87},{4,64},{5,49},{6,34},{7,19},{8,12},{9... | collective-permute-start | bytes 442376 | tf_op jit(solution)/shard_map/ppermute | solution.py:267
  110.2 11.9 %collective-permute-start.25 = (bf16[288,256]{1,0:T(8,128)(2,1)S(1)}, bf16[288,256]{1,0:T(8,128)(2,1)S(1)}, u32[]{:S(2)}, u32[]{:S(2)}) collective-permute-start(bf16[288,256]{1,0:T(8,128)(2,1)S(1)} %get-tuple-element.106), channel_id=1, source_target_pairs={{0,5},{1,118},{2,103},{3,80},{4,65},{5,50},{6,35},{7,20},{8,13},{9... | collective-permute-start | bytes 442376 | tf_op jit(solution)/shard_map/ppermute | solution.py:267
  111.6 17.0 %collective-permute-start.26 = (bf16[288,256]{1,0:T(8,128)(2,1)S(1)}, bf16[288,256]{1,0:T(8,128)(2,1)S(1)}, u32[]{:S(2)}, u32[]{:S(2)}) collective-permute-start(bf16[288,256]{1,0:T(8,128)(2,1)S(1)} %get-tuple-element.107), channel_id=1, source_target_pairs={{0,6},{1,119},{2,96},{3,81},{4,66},{5,51},{6,36},{7,21},{8,14},{9,... | collective-permute-start | bytes 442376 | tf_op jit(solution)/shard_map/ppermute | solution.py:267
  118.3 10.2 %collective-permute-start.27 = (bf16[288,256]{1,0:T(8,128)(2,1)S(1)}, bf16[288,256]{1,0:T(8,128)(2,1)S(1)}, u32[]{:S(2)}, u32[]{:S(2)}) collective-permute-start(bf16[288,256]{1,0:T(8,128)(2,1)S(1)} %get-tuple-element.108), channel_id=1, source_target_pairs={{0,7},{1,112},{2,97},{3,82},{4,67},{5,52},{6,37},{7,22},{8,15},{9,... | collective-permute-start | bytes 442376 | tf_op jit(solution)/shard_map/ppermute | solution.py:267
  (10 other events, 61.5 us)

commit v4 on v3

--- a/solution.py
+++ b/solution.py
@@ -214,7 +214,7 @@
     )(own, first, second, strips)
 
 
-def finish_kernel(scale, *refs):
+def finish_kernel(scale, order, *refs):
     got, (home, whole) = refs[:-2], refs[-2:]
     replica, _ = place_of()
     width = whole.shape[0]
@@ -223,15 +223,15 @@
     for part in got[1:]:
         total += part[:width, :].astype(jnp.float32)
     home[...] = total.T.astype(home.dtype)
-    for d, part in enumerate(got):
+    for d, part in zip(order, got):
         at = pl.multiple_of(lax.rem(replica + len(got) - d, len(got)) * some, some)
         whole[pl.ds(at, some), :] = part[width:, :].astype(jnp.float32) * scale
 
 
-def finish(scale, width, got):
+def finish(scale, width, order, got):
     share = got[0].shape[1]
     return pl.pallas_call(
-        functools.partial(finish_kernel, scale),
+        functools.partial(finish_kernel, scale, order),
         in_specs=[VMEM] * len(got),
         out_specs=[VMEM, VMEM],
         out_shape=[
@@ -343,8 +343,9 @@
     strips = lax.all_to_all(strips + moved(strips, lambda i, r: (i ^ 1, r)), ("row", "rep"), 0, 0, axis_index_groups=same_core)
 
     merged = merge(own, first, second, strips)
-    got = [moved(merged[d], lambda i, r, d=d: (i - sections * r, r + d)) for d in shares]
-    feature_grad, whole = finish(1.0 / math.sqrt(features.shape[0] * rows_n), width, got)
+    order = (7, 6, 5, 4, 3, 2, 1, 0)
+    found = {d: moved(merged[d], lambda i, r, d=d: (i - sections * r, r + d)) for d in order}
+    feature_grad, whole = finish(1.0 / math.sqrt(features.shape[0] * rows_n), width, order, [found[d] for d in order])
     return activated, whole, feature_grad
 
 

time: 130 us -> 129 us (level)
  the two profiles are of different devices: /device:TPU:8 before, /device:TPU:0 now
where the time goes in v4:
time: 129 us
  starting transfers between devices  71.3 us (55%)
  waiting for transfers between devices  23.6 us (18%)
  Pallas kernels  20.4 us (16%)
  blocking collectives  10.5 us (8%)
  local copies, waits for them, and re-layouts  2.03 us (2%)
    ppermute x25, starting transfers between devices, moved(): return lax.ppermute(value, ('row', 'rep'), pairs(rows_n, reps, target))  55.7 us
    ppermute x25, waiting for transfers between devices, moved(): return lax.ppermute(value, ('row', 'rep'), pairs(rows_n, reps, target))  23 us
    ppermute x1, starting transfers between devices, to_other_core(): lax.ppermute(value, ('row', 'rep'), [((i - 1) * reps + r, i * reps + r) f...  12.4 us
    pallas_call x9, Pallas kernels, with_panels(): pl.pallas_call(kernel, in_specs=[VMEM] * (1 + len(operands)), out_specs=[...  10.9 us
    all_to_all x1, blocking collectives, per_device(): lax.all_to_all(strips + moved(strips, lambda i, r: (i ^ 1, r)), ('row', '...  10.5 us
    pallas_call x2, Pallas kernels, build(): pl.pallas_call(functools.partial(build_kernel, part), grid_spec=pltpu.Pre...  8.41 us
    ppermute x2, starting transfers between devices, fetched(): return lax.ppermute(value, ('row', 'rep'), found)  3.18 us
  transfers between devices with their start and end apart: 28, of which 14 were waited for; matrix products, arithmetic and copies ran while one was open for 0% of the time, Pallas kernels for 13%

profile of v4, /device:TPU:0, one launch (start us, length us, event | category | flops | bytes accessed | tf_op | source)
XLA Modules:
  0.0 128.6 jit_solution(320716835781554320)
XLA Ops:
  4.5 4.2 %build.2 = (bf16[2,16,2048,128]{3,2,1,0:T(8,128)(2,1)S(1)}, s32[8,128]{1,0:T(8,128)S(1)}) custom-call(s32[2,192]{1,0:T(2,128)S(1)} %bitcast.5, s32[2,192]{1,0:T(2,128)S(1)} %bitcast.7, s32[2]{0:T(128)S(1)} %bitcast.9, bf16[2,192,128,128]{3,2,1,0:T(8,128)(2,1)} %bitcast.12), custom_call_target="tpu_custom_call" | custom-call | bytes 15728640 | tf_op jit(solution)/shard_map/build/pallas_call | solution.py:57
  10.0 4.2 %build.3 = (bf16[2,16,2048,128]{3,2,1,0:T(8,128)(2,1)S(1)}, s32[8,128]{1,0:T(8,128)S(1)}) custom-call(s32[2,192]{1,0:T(2,128)S(1)} %bitcast.6, s32[2,192]{1,0:T(2,128)S(1)} %bitcast.8, s32[2]{0:T(128)S(1)} %bitcast.10, bf16[2,192,128,128]{3,2,1,0:T(8,128)(2,1)} %bitcast.13, ...), custom_call_target="tpu_custom_call", output_to_operand_aliasing={{0}: (4, {})} | custom-call | bytes 15728640 | tf_op jit(solution)/shard_map/build/pallas_call | solution.py:57
  14.3 12.4 %collective-permute-start.1 = (bf16[2048,256]{1,0:T(8,128)(2,1)S(1)}, bf16[2048,256]{1,0:T(8,128)(2,1)S(1)}, u32[]{:S(2)}, u32[]{:S(2)}) collective-permute-start(bf16[2048,256]{1,0:T(8,128)(2,1)S(1)} %collective-permute-done.source), channel_id=1, source_target_pairs={{0,8},{1,9},{2,10},{3,11},{4,12},{5,13},{6,14},{7,15},{16,24},{17,... | collective-permute-start | bytes 3145736 | tf_op jit(solution)/shard_map/ppermute | solution.py:279
  26.6 2.3 %first.1 = (bf16[2,16,2048,128]{3,2,1,0:T(8,128)(2,1)S(1)}, f32[8,256,256]{2,1,0:T(8,128)S(1)}) custom-call(bf16[2,16,2048,128]{3,2,1,0:T(8,128)(2,1)S(1)} %get-tuple-element.60.panels, bf16[2048,256]{1,0:T(8,128)(2,1)S(1)} %collective-permute-done.source, s32[8,128]{1,0:T(8,128)S(1)} %get-tuple-element.63.token), custom_call_target="tpu_custom_call", output_to_operand_aliasing={{0}: (0, {})} | custom-call | flops 2147483648 | bytes 2097152 | tf_op jit(solution)/shard_map/first/pallas_call | solution.py:81
  30.9 8.0 %collective-permute-start.3 = (bf16[256,256]{1,0:T(8,128)(2,1)S(1)}, bf16[256,256]{1,0:T(8,128)(2,1)S(1)}, u32[]{:S(2)}, u32[]{:S(2)}) collective-permute-start(bf16[256,256]{1,0:T(8,128)(2,1)S(1)} %get-tuple-element.69), channel_id=1, source_target_pairs={{0,1},{1,2},{2,3},{3,4},{4,5},{5,6},{6,7},{7,0},{8,9},{9,10},{10,1... | collective-permute-start | bytes 393224 | tf_op jit(solution)/shard_map/ppermute | solution.py:267
  38.8 3.2 %collective-permute-start.4 = (bf16[256,256]{1,0:T(8,128)(2,1)S(1)}, bf16[256,256]{1,0:T(8,128)(2,1)S(1)}, u32[]{:S(2)}, u32[]{:S(2)}) collective-permute-start(bf16[256,256]{1,0:T(8,128)(2,1)S(1)} %get-tuple-element.70), channel_id=1, source_target_pairs={{0,2},{1,3},{2,4},{3,5},{4,6},{5,7},{6,0},{7,1},{8,10},{9,11},{10,... | collective-permute-start | bytes 393224 | tf_op jit(solution)/shard_map/ppermute | solution.py:267
  43.4 3.2 %collective-permute-start.5 = (bf16[256,256]{1,0:T(8,128)(2,1)S(1)}, bf16[256,256]{1,0:T(8,128)(2,1)S(1)}, u32[]{:S(2)}, u32[]{:S(2)}) collective-permute-start(bf16[256,256]{1,0:T(8,128)(2,1)S(1)} %get-tuple-element.71), channel_id=1, source_target_pairs={{0,3},{1,4},{2,5},{3,6},{4,7},{5,0},{6,1},{7,2},{8,11},{9,12},{10,... | collective-permute-start | bytes 393224 | tf_op jit(solution)/shard_map/ppermute | solution.py:267
  49.9 2.1 %collective-permute-done.5.refs_2_ = bf16[256,256]{1,0:T(8,128)(2,1)S(1)} collective-permute-done((bf16[256,256]{1,0:T(8,128)(2,1)S(1)}, bf16[256,256]{1,0:T(8,128)(2,1)S(1)}, u32[]{:S(2)}, u32[]{:S(2)}) %collective-permute-start.5) | collective-permute-done | bytes 131104 | tf_op jit(solution)/shard_map/ppermute | solution.py:267
  56.9 4.0 %collective-permute-start.11 = (bf16[288,256]{1,0:T(8,128)(2,1)S(1)}, bf16[288,256]{1,0:T(8,128)(2,1)S(1)}, u32[]{:S(2)}, u32[]{:S(2)}) collective-permute-start(bf16[288,256]{1,0:T(8,128)(2,1)S(1)} %get-tuple-element.83), channel_id=1, source_target_pairs={{0,2},{1,3},{2,4},{3,5},{4,6},{5,7},{6,0},{7,1},{8,10},{9,11},{10,... | collective-permute-start | bytes 442376 | tf_op jit(solution)/shard_map/ppermute | solution.py:267
  60.9 3.0 %collective-permute-start.12 = (bf16[288,256]{1,0:T(8,128)(2,1)S(1)}, bf16[288,256]{1,0:T(8,128)(2,1)S(1)}, u32[]{:S(2)}, u32[]{:S(2)}) collective-permute-start(bf16[288,256]{1,0:T(8,128)(2,1)S(1)} %get-tuple-element.84), channel_id=1, source_target_pairs={{0,3},{1,4},{2,5},{3,6},{4,7},{5,0},{6,1},{7,2},{8,11},{9,12},{10,... | collective-permute-start | bytes 442376 | tf_op jit(solution)/shard_map/ppermute | solution.py:267
  63.8 2.1 %collective-permute-start.14 = (bf16[288,256]{1,0:T(8,128)(2,1)S(1)}, bf16[288,256]{1,0:T(8,128)(2,1)S(1)}, u32[]{:S(2)}, u32[]{:S(2)}) collective-permute-start(bf16[288,256]{1,0:T(8,128)(2,1)S(1)} %get-tuple-element.88), channel_id=1, source_target_pairs={{0,5},{1,6},{2,7},{3,0},{4,1},{5,2},{6,3},{7,4},{8,13},{9,14},{10,... | collective-permute-start | bytes 442376 | tf_op jit(solution)/shard_map/ppermute | solution.py:267
  66.0 5.1 %collective-permute-start.15 = (bf16[288,256]{1,0:T(8,128)(2,1)S(1)}, bf16[288,256]{1,0:T(8,128)(2,1)S(1)}, u32[]{:S(2)}, u32[]{:S(2)}) collective-permute-start(bf16[288,256]{1,0:T(8,128)(2,1)S(1)} %get-tuple-element.89), channel_id=1, source_target_pairs={{0,6},{1,7},{2,0},{3,1},{4,2},{5,3},{6,4},{7,5},{8,14},{9,15},{10,... | collective-permute-start | bytes 442376 | tf_op jit(solution)/shard_map/ppermute | solution.py:267
  71.2 2.3 %heads.1 = (bf16[2,16,2048,128]{3,2,1,0:T(8,128)(2,1)S(1)}, f32[8,256,256]{2,1,0:T(8,128)S(1)}, f32[8,256,256]{2,1,0:T(8,128)S(1)}) custom-call(bf16[2,16,2048,128]{3,2,1,0:T(8,128)(2,1)S(1)} %get-tuple-element.80.panels, bf16[256,256]{1,0:T(8,128)(2,1)S(1)} %get-tuple-element.81.refs_0_, ...), custom_call_target="tpu_custom_call", output_to_operand_aliasing={{0}: (0, {})} | custom-call | flops 2147483648 | bytes 2097152 | tf_op jit(solution)/shard_map/heads/pallas_call | solution.py:81
  74.1 2.1 %collective-permute-done.16.refs_3_ = bf16[288,256]{1,0:T(8,128)(2,1)S(1)} collective-permute-done((bf16[288,256]{1,0:T(8,128)(2,1)S(1)}, bf16[288,256]{1,0:T(8,128)(2,1)S(1)}, u32[]{:S(2)}, u32[]{:S(2)}) %collective-permute-start.16) | collective-permute-done | bytes 147488 | tf_op jit(solution)/shard_map/ppermute | solution.py:267
  77.9 5.2 %collective-permute-start.18 = (bf16[4,256,256]{2,1,0:T(8,128)(2,1)S(1)}, bf16[4,256,256]{2,1,0:T(8,128)(2,1)S(1)}, u32[]{:S(2)}, u32[]{:S(2)}) collective-permute-start(bf16[4,256,256]{2,1,0:T(8,128)(2,1)S(1)} %get-tuple-element.99), channel_id=1, source_target_pairs={{0,120},{1,121},{2,122},{3,123},{4,124},{5,125},{6,126},{7,127},{8... | collective-permute-start | bytes 1572872 | tf_op jit(solution)/shard_map/ppermute | solution.py:267
  85.8 10.5 %all_to_all.5.strips = bf16[8,32,256]{2,1,0:T(8,128)(2,1)S(1)} all-to-all(bf16[8,32,256]{2,1,0:T(8,128)(2,1)S(1)} %add.3), channel_id=1, replica_groups={{0,16,32,48,64,80,96,112},{1,17,33,49,65,81,97,113},{2,18,34,50,66,82,9..., dimensions={0} | all-to-all | bytes 262144 | tf_op jit(solution)/shard_map/all_to_all | solution.py:343
  96.5 3.2 %collective-permute-start.20 = (bf16[288,256]{1,0:T(8,128)(2,1)S(1)}, bf16[288,256]{1,0:T(8,128)(2,1)S(1)}, u32[]{:S(2)}, u32[]{:S(2)}) collective-permute-start(bf16[288,256]{1,0:T(8,128)(2,1)S(1)} %get-tuple-element.101), channel_id=1, source_target_pairs={{0,7},{1,112},{2,97},{3,82},{4,67},{5,52},{6,37},{7,22},{8,15},{9,... | collective-permute-start | bytes 442376 | tf_op jit(solution)/shard_map/ppermute | solution.py:267
  99.7 3.5 %collective-permute-start.22 = (bf16[288,256]{1,0:T(8,128)(2,1)S(1)}, bf16[288,256]{1,0:T(8,128)(2,1)S(1)}, u32[]{:S(2)}, u32[]{:S(2)}) collective-permute-start(bf16[288,256]{1,0:T(8,128)(2,1)S(1)} %get-tuple-element.103), channel_id=1, source_target_pairs={{0,5},{1,118},{2,103},{3,80},{4,65},{5,50},{6,35},{7,20},{8,13},{9... | collective-permute-start | bytes 442376 | tf_op jit(solution)/shard_map/ppermute | solution.py:267
  103.2 2.7 %collective-permute-start.23 = (bf16[288,256]{1,0:T(8,128)(2,1)S(1)}, bf16[288,256]{1,0:T(8,128)(2,1)S(1)}, u32[]{:S(2)}, u32[]{:S(2)}) collective-permute-start(bf16[288,256]{1,0:T(8,128)(2,1)S(1)} %get-tuple-element.104), channel_id=1, source_target_pairs={{0,4},{1,117},{2,102},{3,87},{4,64},{5,49},{6,34},{7,19},{8,12},{9... | collective-permute-start | bytes 442376 | tf_op jit(solution)/shard_map/ppermute | solution.py:267
  105.9 4.5 %collective-permute-start.24 = (bf16[288,256]{1,0:T(8,128)(2,1)S(1)}, bf16[288,256]{1,0:T(8,128)(2,1)S(1)}, u32[]{:S(2)}, u32[]{:S(2)}) collective-permute-start(bf16[288,256]{1,0:T(8,128)(2,1)S(1)} %get-tuple-element.105), channel_id=1, source_target_pairs={{0,3},{1,116},{2,101},{3,86},{4,71},{5,48},{6,33},{7,18},{8,11},{9... | collective-permute-start | bytes 442376 | tf_op jit(solution)/shard_map/ppermute | solution.py:267
  110.7 3.3 %collective-permute-start.26 = (bf16[288,256]{1,0:T(8,128)(2,1)S(1)}, bf16[288,256]{1,0:T(8,128)(2,1)S(1)}, u32[]{:S(2)}, u32[]{:S(2)}) collective-permute-start(bf16[288,256]{1,0:T(8,128)(2,1)S(1)} %get-tuple-element.107), channel_id=1, source_target_pairs={{0,1},{1,114},{2,99},{3,84},{4,69},{5,54},{6,39},{7,16},{8,9},{9,1... | collective-permute-start | bytes 442376 | tf_op jit(solution)/shard_map/ppermute | solution.py:267
  117.1 3.4 %collective-permute-done.24.refs_4_ = bf16[288,256]{1,0:T(8,128)(2,1)S(1)} collective-permute-done((bf16[288,256]{1,0:T(8,128)(2,1)S(1)}, bf16[288,256]{1,0:T(8,128)(2,1)S(1)}, u32[]{:S(2)}, u32[]{:S(2)}) %collective-permute-start.24) | collective-permute-done | bytes 147488 | tf_op jit(solution)/shard_map/ppermute | solution.py:267
  120.4 3.9 %collective-permute-done.25.refs_5_ = bf16[288,256]{1,0:T(8,128)(2,1)S(1)} collective-permute-done((bf16[288,256]{1,0:T(8,128)(2,1)S(1)}, bf16[288,256]{1,0:T(8,128)(2,1)S(1)}, u32[]{:S(2)}, u32[]{:S(2)}) %collective-permute-start.25) | collective-permute-done | bytes 147488 | tf_op jit(solution)/shard_map/ppermute | solution.py:267
  124.3 3.4 %collective-permute-done.26.refs_6_ = bf16[288,256]{1,0:T(8,128)(2,1)S(1)} collective-permute-done((bf16[288,256]{1,0:T(8,128)(2,1)S(1)}, bf16[288,256]{1,0:T(8,128)(2,1)S(1)}, u32[]{:S(2)}, u32[]{:S(2)}) %collective-permute-start.26) | collective-permute-done | bytes 147488 | tf_op jit(solution)/shard_map/ppermute | solution.py:267
  (59 shorter events, 26.1 us)
Async XLA Ops:
  0.6 13.6 %collective-permute-start = (bf16[2048,256]{1,0:T(8,128)(2,1)}, bf16[2048,256]{1,0:T(8,128)(2,1)S(1)}, u32[]{:S(2)}, u32[]{:S(2)}) collective-permute-start(bf16[2048,256]{1,0:T(8,128)(2,1)} %param.8), channel_id=1, source_target_pairs={{0,0},{117,1},{98,2},{87,3},{68,4},{49,5},{38,6},{19,7},{8,8},{125... | collective-permute-start | bytes 3145736 | tf_op jit(solution)/shard_map/ppermute | solution.py:276
  8.7 20.8 %collective-permute-start.2 = (bf16[2048,256]{1,0:T(8,128)(2,1)}, bf16[2048,256]{1,0:T(8,128)(2,1)S(1)}, u32[]{:S(2)}, u32[]{:S(2)}) collective-permute-start(bf16[2048,256]{1,0:T(8,128)(2,1)} %param.8), channel_id=1, source_target_pairs={{121,0},{110,1},{91,2},{72,3},{61,4},{42,5},{31,6},{12,7},{9,16},{... | collective-permute-start | bytes 3145736 | tf_op jit(solution)/shard_map/ppermute | solution.py:276
  14.3 15.3 %collective-permute-start.1 = (bf16[2048,256]{1,0:T(8,128)(2,1)S(1)}, bf16[2048,256]{1,0:T(8,128)(2,1)S(1)}, u32[]{:S(2)}, u32[]{:S(2)}) collective-permute-start(bf16[2048,256]{1,0:T(8,128)(2,1)S(1)} %collective-permute-done.source), channel_id=1, source_target_pairs={{0,8},{1,9},{2,10},{3,11},{4,12},{5,13},{6,14},{7,15},{16,24},{17,... | collective-permute-start | bytes 3145736 | tf_op jit(solution)/shard_map/ppermute | solution.py:279
  30.9 15.7 %collective-permute-start.3 = (bf16[256,256]{1,0:T(8,128)(2,1)S(1)}, bf16[256,256]{1,0:T(8,128)(2,1)S(1)}, u32[]{:S(2)}, u32[]{:S(2)}) collective-permute-start(bf16[256,256]{1,0:T(8,128)(2,1)S(1)} %get-tuple-element.69), channel_id=1, source_target_pairs={{0,1},{1,2},{2,3},{3,4},{4,5},{5,6},{6,7},{7,0},{8,9},{9,10},{10,1... | collective-permute-start | bytes 393224 | tf_op jit(solution)/shard_map/ppermute | solution.py:267
  38.8 9.3 %collective-permute-start.4 = (bf16[256,256]{1,0:T(8,128)(2,1)S(1)}, bf16[256,256]{1,0:T(8,128)(2,1)S(1)}, u32[]{:S(2)}, u32[]{:S(2)}) collective-permute-start(bf16[256,256]{1,0:T(8,128)(2,1)S(1)} %get-tuple-element.70), channel_id=1, source_target_pairs={{0,2},{1,3},{2,4},{3,5},{4,6},{5,7},{6,0},{7,1},{8,10},{9,11},{10,... | collective-permute-start | bytes 393224 | tf_op jit(solution)/shard_map/ppermute | solution.py:267
  43.3 9.6 %collective-permute-start.7 = (bf16[256,256]{1,0:T(8,128)(2,1)S(1)}, bf16[256,256]{1,0:T(8,128)(2,1)S(1)}, u32[]{:S(2)}, u32[]{:S(2)}) collective-permute-start(bf16[256,256]{1,0:T(8,128)(2,1)S(1)} %get-tuple-element.76), channel_id=1, source_target_pairs={{0,5},{1,6},{2,7},{3,0},{4,1},{5,2},{6,3},{7,4},{8,13},{9,14},{10,... | collective-permute-start | bytes 393224 | tf_op jit(solution)/shard_map/ppermute | solution.py:267
  43.4 8.7 %collective-permute-start.5 = (bf16[256,256]{1,0:T(8,128)(2,1)S(1)}, bf16[256,256]{1,0:T(8,128)(2,1)S(1)}, u32[]{:S(2)}, u32[]{:S(2)}) collective-permute-start(bf16[256,256]{1,0:T(8,128)(2,1)S(1)} %get-tuple-element.71), channel_id=1, source_target_pairs={{0,3},{1,4},{2,5},{3,6},{4,7},{5,0},{6,1},{7,2},{8,11},{9,12},{10,... | collective-permute-start | bytes 393224 | tf_op jit(solution)/shard_map/ppermute | solution.py:267
  46.6 7.5 %collective-permute-start.8 = (bf16[256,256]{1,0:T(8,128)(2,1)S(1)}, bf16[256,256]{1,0:T(8,128)(2,1)S(1)}, u32[]{:S(2)}, u32[]{:S(2)}) collective-permute-start(bf16[256,256]{1,0:T(8,128)(2,1)S(1)} %get-tuple-element.77), channel_id=1, source_target_pairs={{0,6},{1,7},{2,0},{3,1},{4,2},{5,3},{6,4},{7,5},{8,14},{9,15},{10,... | collective-permute-start | bytes 393224 | tf_op jit(solution)/shard_map/ppermute | solution.py:267
  56.5 9.5 %collective-permute-start.10 = (bf16[288,256]{1,0:T(8,128)(2,1)S(1)}, bf16[288,256]{1,0:T(8,128)(2,1)S(1)}, u32[]{:S(2)}, u32[]{:S(2)}) collective-permute-start(bf16[288,256]{1,0:T(8,128)(2,1)S(1)} %get-tuple-element.82), channel_id=1, source_target_pairs={{0,1},{1,2},{2,3},{3,4},{4,5},{5,6},{6,7},{7,0},{8,9},{9,10},{10,1... | collective-permute-start | bytes 442376 | tf_op jit(solution)/shard_map/ppermute | solution.py:267
  56.9 14.2 %collective-permute-start.11 = (bf16[288,256]{1,0:T(8,128)(2,1)S(1)}, bf16[288,256]{1,0:T(8,128)(2,1)S(1)}, u32[]{:S(2)}, u32[]{:S(2)}) collective-permute-start(bf16[288,256]{1,0:T(8,128)(2,1)S(1)} %get-tuple-element.83), channel_id=1, source_target_pairs={{0,2},{1,3},{2,4},{3,5},{4,6},{5,7},{6,0},{7,1},{8,10},{9,11},{10,... | collective-permute-start | bytes 442376 | tf_op jit(solution)/shard_map/ppermute | solution.py:267
  60.9 10.3 %collective-permute-start.12 = (bf16[288,256]{1,0:T(8,128)(2,1)S(1)}, bf16[288,256]{1,0:T(8,128)(2,1)S(1)}, u32[]{:S(2)}, u32[]{:S(2)}) collective-permute-start(bf16[288,256]{1,0:T(8,128)(2,1)S(1)} %get-tuple-element.84), channel_id=1, source_target_pairs={{0,3},{1,4},{2,5},{3,6},{4,7},{5,0},{6,1},{7,2},{8,11},{9,12},{10,... | collective-permute-start | bytes 442376 | tf_op jit(solution)/shard_map/ppermute | solution.py:267
  63.8 9.8 %collective-permute-start.13 = (bf16[288,256]{1,0:T(8,128)(2,1)S(1)}, bf16[288,256]{1,0:T(8,128)(2,1)S(1)}, u32[]{:S(2)}, u32[]{:S(2)}) collective-permute-start(bf16[288,256]{1,0:T(8,128)(2,1)S(1)} %get-tuple-element.87), channel_id=1, source_target_pairs={{0,4},{1,5},{2,6},{3,7},{4,0},{5,1},{6,2},{7,3},{8,12},{9,13},{10,... | collective-permute-start | bytes 442376 | tf_op jit(solution)/shard_map/ppermute | solution.py:267
  63.8 9.8 %collective-permute-start.14 = (bf16[288,256]{1,0:T(8,128)(2,1)S(1)}, bf16[288,256]{1,0:T(8,128)(2,1)S(1)}, u32[]{:S(2)}, u32[]{:S(2)}) collective-permute-start(bf16[288,256]{1,0:T(8,128)(2,1)S(1)} %get-tuple-element.88), channel_id=1, source_target_pairs={{0,5},{1,6},{2,7},{3,0},{4,1},{5,2},{6,3},{7,4},{8,13},{9,14},{10,... | collective-permute-start | bytes 442376 | tf_op jit(solution)/shard_map/ppermute | solution.py:267
  66.0 8.1 %collective-permute-start.15 = (bf16[288,256]{1,0:T(8,128)(2,1)S(1)}, bf16[288,256]{1,0:T(8,128)(2,1)S(1)}, u32[]{:S(2)}, u32[]{:S(2)}) collective-permute-start(bf16[288,256]{1,0:T(8,128)(2,1)S(1)} %get-tuple-element.89), channel_id=1, source_target_pairs={{0,6},{1,7},{2,0},{3,1},{4,2},{5,3},{6,4},{7,5},{8,14},{9,15},{10,... | collective-permute-start | bytes 442376 | tf_op jit(solution)/shard_map/ppermute | solution.py:267
  76.9 19.3 %collective-permute-start.17 = (bf16[4,256,256]{2,1,0:T(8,128)(2,1)S(1)}, bf16[4,256,256]{2,1,0:T(8,128)(2,1)S(1)}, u32[]{:S(2)}, u32[]{:S(2)}) collective-permute-start(bf16[4,256,256]{2,1,0:T(8,128)(2,1)S(1)} %get-tuple-element.98), channel_id=1, source_target_pairs={{0,9},{1,10},{2,11},{3,12},{4,13},{5,14},{6,15},{7,8},{8,0},{9,1},... | collective-permute-start | bytes 1572872 | tf_op jit(solution)/shard_map/ppermute | solution.py:267
  77.9 18.4 %collective-permute-start.18 = (bf16[4,256,256]{2,1,0:T(8,128)(2,1)S(1)}, bf16[4,256,256]{2,1,0:T(8,128)(2,1)S(1)}, u32[]{:S(2)}, u32[]{:S(2)}) collective-permute-start(bf16[4,256,256]{2,1,0:T(8,128)(2,1)S(1)} %get-tuple-element.99), channel_id=1, source_target_pairs={{0,120},{1,121},{2,122},{3,123},{4,124},{5,125},{6,126},{7,127},{8... | collective-permute-start | bytes 1572872 | tf_op jit(solution)/shard_map/ppermute | solution.py:267
  96.5 13.9 %collective-permute-start.20 = (bf16[288,256]{1,0:T(8,128)(2,1)S(1)}, bf16[288,256]{1,0:T(8,128)(2,1)S(1)}, u32[]{:S(2)}, u32[]{:S(2)}) collective-permute-start(bf16[288,256]{1,0:T(8,128)(2,1)S(1)} %get-tuple-element.101), channel_id=1, source_target_pairs={{0,7},{1,112},{2,97},{3,82},{4,67},{5,52},{6,37},{7,22},{8,15},{9,... | collective-permute-start | bytes 442376 | tf_op jit(solution)/shard_map/ppermute | solution.py:267
  99.7 11.0 %collective-permute-start.21 = (bf16[288,256]{1,0:T(8,128)(2,1)S(1)}, bf16[288,256]{1,0:T(8,128)(2,1)S(1)}, u32[]{:S(2)}, u32[]{:S(2)}) collective-permute-start(bf16[288,256]{1,0:T(8,128)(2,1)S(1)} %get-tuple-element.102), channel_id=1, source_target_pairs={{0,6},{1,119},{2,96},{3,81},{4,66},{5,51},{6,36},{7,21},{8,14},{9,... | collective-permute-start | bytes 442376 | tf_op jit(solution)/shard_map/ppermute | solution.py:267
  99.7 14.9 %collective-permute-start.22 = (bf16[288,256]{1,0:T(8,128)(2,1)S(1)}, bf16[288,256]{1,0:T(8,128)(2,1)S(1)}, u32[]{:S(2)}, u32[]{:S(2)}) collective-permute-start(bf16[288,256]{1,0:T(8,128)(2,1)S(1)} %get-tuple-element.103), channel_id=1, source_target_pairs={{0,5},{1,118},{2,103},{3,80},{4,65},{5,50},{6,35},{7,20},{8,13},{9... | collective-permute-start | bytes 442376 | tf_op jit(solution)/shard_map/ppermute | solution.py:267
  103.2 13.8 %collective-permute-start.23 = (bf16[288,256]{1,0:T(8,128)(2,1)S(1)}, bf16[288,256]{1,0:T(8,128)(2,1)S(1)}, u32[]{:S(2)}, u32[]{:S(2)}) collective-permute-start(bf16[288,256]{1,0:T(8,128)(2,1)S(1)} %get-tuple-element.104), channel_id=1, source_target_pairs={{0,4},{1,117},{2,102},{3,87},{4,64},{5,49},{6,34},{7,19},{8,12},{9... | collective-permute-start | bytes 442376 | tf_op jit(solution)/shard_map/ppermute | solution.py:267
  105.9 14.5 %collective-permute-start.24 = (bf16[288,256]{1,0:T(8,128)(2,1)S(1)}, bf16[288,256]{1,0:T(8,128)(2,1)S(1)}, u32[]{:S(2)}, u32[]{:S(2)}) collective-permute-start(bf16[288,256]{1,0:T(8,128)(2,1)S(1)} %get-tuple-element.105), channel_id=1, source_target_pairs={{0,3},{1,116},{2,101},{3,86},{4,71},{5,48},{6,33},{7,18},{8,11},{9... | collective-permute-start | bytes 442376 | tf_op jit(solution)/shard_map/ppermute | solution.py:267
  110.5 13.8 %collective-permute-start.25 = (bf16[288,256]{1,0:T(8,128)(2,1)S(1)}, bf16[288,256]{1,0:T(8,128)(2,1)S(1)}, u32[]{:S(2)}, u32[]{:S(2)}) collective-permute-start(bf16[288,256]{1,0:T(8,128)(2,1)S(1)} %get-tuple-element.106), channel_id=1, source_target_pairs={{0,2},{1,115},{2,100},{3,85},{4,70},{5,55},{6,32},{7,17},{8,10},{9... | collective-permute-start | bytes 442376 | tf_op jit(solution)/shard_map/ppermute | solution.py:267
  110.7 17.0 %collective-permute-start.26 = (bf16[288,256]{1,0:T(8,128)(2,1)S(1)}, bf16[288,256]{1,0:T(8,128)(2,1)S(1)}, u32[]{:S(2)}, u32[]{:S(2)}) collective-permute-start(bf16[288,256]{1,0:T(8,128)(2,1)S(1)} %get-tuple-element.107), channel_id=1, source_target_pairs={{0,1},{1,114},{2,99},{3,84},{4,69},{5,54},{6,39},{7,16},{8,9},{9,1... | collective-permute-start | bytes 442376 | tf_op jit(solution)/shard_map/ppermute | solution.py:267
  114.6 13.1 %collective-permute-start.27 = (bf16[288,256]{1,0:T(8,128)(2,1)S(1)}, bf16[288,256]{1,0:T(8,128)(2,1)S(1)}, u32[]{:S(2)}, u32[]{:S(2)}) collective-permute-start(bf16[288,256]{1,0:T(8,128)(2,1)S(1)} %get-tuple-element.108), channel_id=1, source_target_pairs={{0,0},{1,113},{2,98},{3,83},{4,68},{5,53},{6,38},{7,23},{8,8},{9,1... | collective-permute-start | bytes 442376 | tf_op jit(solution)/shard_map/ppermute | solution.py:267
  (10 other events, 62.8 us)
